TPU v7x, 512 devices: a whole 4x4x16 slice. The times are simulated.
512 devices in a mesh: dp: 64 (over y, z), group: 8 (over x, core).
Axes of the slice: x: 4, y: 4, z: 16, core: 2. Of those that a mesh axis runs over, the one named last changes fastest.
Arguments:
- queries: bfloat16 [8, 8192, 4096], P('group', 'dp'), may hold values from -6 to 6
- out_grad: bfloat16 [8, 8192, 4096], P('group', 'dp')
- keys_values: bfloat16 [8, 8192, 1024], P('group', 'dp'), may hold values from -6 to 6
- prompt_kv: bfloat16 [8, 4096, 1024], P('group', 'dp'), may hold values from -6 to 6
- q_gain: float32 [128], replicated, may hold values from 0.5 to 1.5
- k_gain: float32 [128], replicated, may hold values from 0.5 to 1.5
- block_owner: int32 [8, 128], P('group', 'dp'), may hold values from 0 to 63, as said below
- block_start: int32 [8, 128], P('group', 'dp'), may hold values 0 or 1
Outputs:
- query_grad: bfloat16 [8, 8192, 4096], P('group', 'dp')
- kv_grad: bfloat16 [8, 8192, 1024], P('group', 'dp')
- prompt_kv_grad: bfloat16 [8, 4096, 1024], P('group', 'dp')
- gain_grads: float32 [2, 128], replicated
Inputs may be any that keep to these rules, and one draw needn't show every extreme that they name: Within a group block_owner never falls from one block to the next; block i (on device i // 2) names a prompt between i // 2 - (3) and i // 2, and in every group some block names the prompt exactly 3 devices before its own.
All inputs are finite; a program needn't handle non-finite values. No bound on the sum of `block_start` on one device may be relied on, other than what follows from the above.
Results may differ from a plain program's by a relative error of at most 0.01.
Values may be sent and summed in bfloat16 or wider, within the bound.
A program may use at most 64 MiB of HBM per device.

v0:
```python
from functools import reduce
import math

import jax
import jax.numpy as jnp
from jax import lax
from jax.sharding import PartitionSpec as P

H = 32
KVH = 4
HD = 128
BLK = 64
NB = 2
SPAN = 4
P_SIZE = 64
QW = 4096
KW = 512
CT = 128


NORM_EPS = 1e-06


def from_behind(shard, axis, by):
    peers = lax.axis_size(axis)
    pairs = [(i, i + by) for i in range(peers) if 0 <= i + by < peers]
    return lax.ppermute(shard, axis, pairs)


def unit_rows(raw_rows):
    return raw_rows * lax.rsqrt(jnp.mean(raw_rows * raw_rows, axis=-1, keepdims=True) + NORM_EPS)


def norm_backward(raw_rows, gain_vector, upstream):
    inverse = lax.rsqrt(jnp.mean(raw_rows * raw_rows, axis=-1, keepdims=True) + NORM_EPS)
    weighted = upstream * gain_vector
    d_raw = inverse * weighted - raw_rows * inverse**3 * jnp.mean(
        raw_rows * weighted, axis=-1, keepdims=True
    )
    d_gain = jnp.sum((raw_rows * inverse * upstream).reshape(-1, raw_rows.shape[-1]), axis=0)
    return (d_raw, d_gain)


def row_segments(owners, starts):
    changed = jnp.concatenate(
        [
            jnp.ones((1,), jnp.int32),
            jnp.maximum(starts[1:], (owners[1:] != owners[:-1]).astype(jnp.int32)),
        ]
    )
    return jnp.repeat(jnp.cumsum(changed), BLK, total_repeat_length=NB * BLK)


def attention_terms(queries, out_grad, keys_values, prefix, segments, q_gain, k_gain):
    members = H // KVH
    score_scale = HD ** (-0.5)
    q_raw = queries.astype(jnp.float32).reshape(CT, KVH, members, HD)
    q_norm = (unit_rows(q_raw) * q_gain).astype(jnp.bfloat16)
    k_raw = keys_values[:, :KW].astype(jnp.float32).reshape(CT, KVH, HD)
    k_norm = (unit_rows(k_raw) * k_gain).astype(jnp.bfloat16)
    values = keys_values[:, KW:].reshape(CT, KVH, HD)
    p_raw = prefix[:, :, :KW].astype(jnp.float32).reshape(NB, P_SIZE, KVH, HD)
    p_norm = (unit_rows(p_raw) * k_gain).astype(jnp.bfloat16)
    p_values = prefix[:, :, KW:].reshape(NB, P_SIZE, KVH, HD)
    key_all = jnp.concatenate([jnp.broadcast_to(k_norm[None], (NB, CT, KVH, HD)), p_norm], axis=1)
    value_all = jnp.concatenate(
        [jnp.broadcast_to(values[None], (NB, CT, KVH, HD)), p_values], axis=1
    )
    q_blocks = q_norm.reshape(NB, BLK, KVH, members, HD)
    out_blocks = out_grad.reshape(NB, BLK, KVH, members, HD)
    scores = (
        jnp.einsum("nbkgd,nskd->nkgbs", q_blocks, key_all, preferred_element_type=jnp.float32)
        * score_scale
    )
    row_index = lax.iota(jnp.int32, CT).reshape(NB, BLK)
    column = lax.iota(jnp.int32, CT + P_SIZE)
    seg_cols = jnp.concatenate([segments, jnp.full((P_SIZE,), -1, jnp.int32)])
    seg_rows = segments.reshape(NB, BLK)
    allowed = (column[None, None, :] >= CT) | (seg_rows[:, :, None] == seg_cols[None, None, :]) & (
        column[None, None, :] <= row_index[:, :, None]
    )
    exps = jnp.where(allowed[:, None, None, :, :], jnp.exp(scores), 0.0)
    totals = jnp.sum(exps, axis=-1, keepdims=True)
    prob = exps / totals
    weight = prob.astype(jnp.bfloat16)
    attended = jnp.einsum(
        "nkgbs,nskd->nbkgd", weight, value_all, preferred_element_type=jnp.float32
    )
    delta = jnp.sum(out_blocks.astype(jnp.float32) * attended, axis=-1).transpose(0, 2, 3, 1)
    d_prob = jnp.einsum(
        "nbkgd,nskd->nkgbs", out_blocks, value_all, preferred_element_type=jnp.float32
    )
    d_score = (prob * (d_prob - delta[..., None])).astype(jnp.bfloat16)
    d_qnorm = (
        jnp.einsum(
            "nkgbs,nskd->nbkgd", d_score, key_all, preferred_element_type=jnp.float32
        ).reshape(CT, KVH, members, HD)
        * score_scale
    )
    d_key_all = (
        jnp.einsum("nkgbs,nbkgd->nskd", d_score, q_blocks, preferred_element_type=jnp.float32)
        * score_scale
    )
    d_value_all = jnp.einsum(
        "nkgbs,nbkgd->nskd", weight, out_blocks, preferred_element_type=jnp.float32
    )
    d_knorm = jnp.sum(d_key_all[:, :CT], axis=0)
    d_values = jnp.sum(d_value_all[:, :CT], axis=0)
    d_pnorm = d_key_all[:, CT:]
    d_pvalues = d_value_all[:, CT:]
    d_query, q_part = norm_backward(q_raw, q_gain, d_qnorm)
    d_key, k_part = norm_backward(k_raw, k_gain, d_knorm)
    query_grad = d_query.reshape(CT, QW).astype(jnp.bfloat16)
    kv_grad = jnp.concatenate([d_key.reshape(CT, KW), d_values.reshape(CT, KW)], axis=1).astype(
        jnp.bfloat16
    )
    prefix_part = jnp.concatenate(
        [d_pnorm.reshape(NB, P_SIZE, KW), d_pvalues.reshape(NB, P_SIZE, KW)], axis=-1
    )
    return (query_grad, kv_grad, prefix_part, q_part, k_part)


def shards(queries, out_grad, keys_values, prompt_kv, q_gain, k_gain, block_owner, block_start):
    own_prompt = prompt_kv[0]
    fetched = [own_prompt] + [
        from_behind(own_prompt, "dp", hop_count) for hop_count in range(1, SPAN)
    ]
    candidates = jnp.stack(fetched)
    owners = block_owner[0]
    slot_index = lax.axis_index("dp") - owners
    prefix = jnp.take(candidates, slot_index, axis=0)
    segments = row_segments(owners, block_start[0])
    query_grad, kv_grad, prefix_part, q_part, k_part = attention_terms(
        queries[0], out_grad[0], keys_values[0], prefix, segments, q_gain, k_gain
    )
    choose = (slot_index[:, None] == lax.iota(jnp.int32, SPAN)[None, :]).astype(jnp.float32)
    by_slot = jnp.einsum("ns,npc->spc", choose, prefix_part, precision=lax.Precision.HIGHEST)
    arrivals = [
        from_behind(by_slot[hop_count].astype(jnp.bfloat16), "dp", -hop_count).astype(jnp.float32)
        for hop_count in range(1, SPAN)
    ]
    summed = reduce(lambda left_sum, right_sum: left_sum + right_sum, arrivals, by_slot[0])
    prompt_raw = own_prompt[:, :KW].astype(jnp.float32).reshape(P_SIZE, KVH, HD)
    d_prompt_key, prompt_part = norm_backward(
        prompt_raw, k_gain, summed[:, :KW].reshape(P_SIZE, KVH, HD)
    )
    prompt_grad = jnp.concatenate(
        [d_prompt_key.reshape(P_SIZE, KW), summed[:, KW:]], axis=1
    ).astype(jnp.bfloat16)
    gain_terms = jnp.stack([q_part, k_part + prompt_part])
    gain_total = lax.psum(gain_terms, ("dp", "group"))
    all_rows = lax.axis_size("dp") * lax.axis_size("group") * CT
    gain_grads = gain_total * (1.0 / math.sqrt(all_rows))
    return (query_grad[None], kv_grad[None], prompt_grad[None], gain_grads)


def solution(mesh):
    placed = (
        P("group", "dp", None),
        P("group", "dp", None),
        P("group", "dp", None),
        P("group", "dp", None),
        P(),
        P(),
        P("group", "dp"),
        P("group", "dp"),
    )
    return jax.shard_map(
        shards,
        mesh=mesh,
        in_specs=placed,
        out_specs=(P("group", "dp", None), P("group", "dp", None), P("group", "dp", None), P()),
        check_vma=False,
    )
```

profile of v0, /device:TPU:1, one launch (start us, length us, event | category | flops | bytes accessed | tf_op | source)
XLA Modules:
  0.0 243.1 jit_solution(4599251580010154051)
XLA Ops:
  0.7 5.2 %collective-permute-start = (bf16[64,1024]{1,0:T(8,128)(2,1)}, bf16[64,1024]{1,0:T(8,128)(2,1)}, u32[]{:S(2)}, u32[]{:S(2)}) collective-permute-start(bf16[64,1024]{1,0:T(8,128)(2,1)} %bitcast.222), channel_id=1, source_target_pairs={{0,8},{8,16},{16,24},{24,32},{32,40},{40,48},{48,56},{56,64},{64,7... | collective-permute-start | bytes 393224 | tf_op jit(solution)/shard_map/ppermute | solution.py:27
  5.8 4.9 %collective-permute-start.1 = (bf16[64,1024]{1,0:T(8,128)(2,1)}, bf16[64,1024]{1,0:T(8,128)(2,1)}, u32[]{:S(2)}, u32[]{:S(2)}) collective-permute-start(bf16[64,1024]{1,0:T(8,128)(2,1)} %bitcast.223), channel_id=1, source_target_pairs={{0,16},{8,24},{16,32},{24,40},{32,48},{40,56},{48,64},{56,72},{64,... | collective-permute-start | bytes 393224 | tf_op jit(solution)/shard_map/ppermute | solution.py:27
  10.7 7.4 %collective-permute-start.2 = (bf16[64,1024]{1,0:T(8,128)(2,1)}, bf16[64,1024]{1,0:T(8,128)(2,1)}, u32[]{:S(2)}, u32[]{:S(2)}) collective-permute-start(bf16[64,1024]{1,0:T(8,128)(2,1)} %bitcast.224), channel_id=1, source_target_pairs={{0,24},{8,32},{16,40},{24,48},{32,56},{40,64},{48,72},{56,80},{64,... | collective-permute-start | bytes 393224 | tf_op jit(solution)/shard_map/ppermute | solution.py:27
  19.1 1.3 fusion.50
  20.4 1.2 compare_and_fusion
  22.9 1.2 slice.76
  25.6 2.0 broadcast_select_fusion.1
  27.6 1.1 copy.245
  37.2 1.5 reshape.477
  40.5 2.4 copy.295
  42.9 1.9 mul.347
  44.9 2.8 %mul.348 = f32[1,128,4096]{2,1,0:T(8,128)} reshape(f32[128,4,8,128]{3,2,1,0:T(8,128)} %mul.347) | data formatting | bytes 4194304 | tf_op jit(solution)/shard_map/mul | solution.py:37
  47.6 1.9 mul.374
  49.6 2.8 %mul.375 = f32[1,128,4096]{2,1,0:T(8,128)} reshape(f32[128,4,8,128]{3,2,1,0:T(8,128)} %mul.374) | data formatting | bytes 4194304 | tf_op jit(solution)/shard_map/mul | solution.py:37
  53.0 1.9 pad_maximum_fusion
  54.9 1.7 gather_fusion
  58.2 1.7 reshape.475
  59.9 1.8 multiply_reduce_fusion.3
  61.7 1.5 copy.251
  63.9 0.9 copy.328
  65.7 3.4 %fusion.3 = (f32[2,4,8,64]{3,2,1,0:T(8,128)S(1)}, f32[2,4,192,64,8]{2,3,4,1,0:T(8,128)S(1)}) fusion(pred[2,64,192]{2,1,0:T(8,128)(4,1)} %fusion.32, f32[2,64,4,8,128]{4,3,2,1,0:T(8,128)S(1)} %bitcast.206, f32[128]{0:T(128)} %param.14, f32[2,64,4,8]{1,3,2,0:T(8,128)} %copy.254, bf16[2,64,4,128]{3,1,2,0:T(8,128)(2,1)S(1)} %fusion.24, ...), kind=kOutput, calls=%fused_computation.6 | convolution fusion | flops 206041088 | bytes 5693952 | tf_op jit(solution)/shard_map/nbkgd,nskd->nkgbs/dot_general | solution.py:72
  69.2 3.0 %convolution_bitcast_fusion.1 = f32[2,192,4,128]{3,1,2,0:T(8,128)} fusion(bf16[2,64,4,8,128]{4,3,2,1,0:T(8,128)(2,1)S(1)} %bitcast.213, f32[2,4,192,64,8]{2,3,4,1,0:T(8,128)S(1)} %get-tuple-element.65, f32[2,4,8,64]{3,2,1,0:T(8,128)S(1)} %get-tuple-element.64, pred[2,64,192]{2,1,0:T(8,128)(4,1)S(1)} %copy-done.28), kind=kOutput, calls=%fused_computation.19 | convolution fusion | flops 204472320 | bytes 5021696 | tf_op jit(solution)/shard_map/nkgbs,nbkgd->nskd/dot_general | solution.py:104
  72.2 1.6 fusion.5
  73.9 1.8 fusion.1
  75.7 2.1 fusion.9
  80.3 3.8 %broadcast_multiply_fusion = (f32[2,64,4,8,128]{4,1,3,2,0:T(8,128)}, f32[2,64,4,8,128]{4,1,3,2,0:T(8,128)S(1)}) fusion(bf16[2,4,8,64,192]{4,3,2,1,0:T(8,128)(2,1)} %copy-done.6, bf16[2,64,4,128]{3,1,2,0:T(8,128)(2,1)S(1)} %copy-done.21, bf16[2,128,4,128]{3,1,2,0:T(8,128)(2,1)} %copy-done.12), kind=kOutput, calls=%fused_computation.24 | convolution fusion | flops 202637312 | bytes 6160384 | tf_op jit(solution)/shard_map/nkgbs,nskd->nbkgd/dot_general | solution.py:95
  84.9 1.2 copy.260
  86.1 1.3 copy-done
  87.4 1.6 bitcast_multiply_fusion.1
  89.0 2.8 %reshape.465 = f32[1,128,4096]{2,1,0:T(8,128)} reshape(f32[2,64,4,8,128]{4,3,2,1,0:T(8,128)} %copy-done) | data formatting | bytes 4194304 | tf_op jit(solution)/shard_map/reshape | solution.py:97
  91.8 0.9 copy.279
  92.7 1.1 reshape.506
  93.8 1.8 copy.280
  95.7 1.8 reshape.507
  97.5 3.6 %fusion.51 = (bf16[4,64,1024]{2,0,1:T(4,128)(2,1)S(1)}, f32[4,64,1024]{2,0,1:T(4,128)}) fusion(f32[2,64,512]{2,0,1:T(2,128)} %reshape.507, f32[2,64,512]{2,0,1:T(2,128)S(1)} %reshape.506, s32[2]{0:T(128)} %get-tuple-element.43), kind=kOutput, calls=%fused_computation.123 | convolution fusion | flops 6684680 | bytes 2097160 | tf_op jit(solution)/shard_map/ns,npc->spc/dot_general | solution.py:137
  102.5 1.3 collective-permute-start.3
  104.5 1.3 collective-permute-start.4
  106.5 1.3 collective-permute-start.5
  108.3 2.5 %copy.271 = f32[2,64,4,8,128]{4,3,2,1,0:T(8,128)} copy(f32[2,64,4,8,128]{4,1,3,2,0:T(8,128)S(1)} %copy-done.5) | data formatting | bytes 4194304 | tf_op jit(solution)/shard_map/mul | solution.py:95
  111.7 2.3 multiply_reduce_fusion
  114.0 1.9 mul.380
  116.0 2.9 %mul.381 = f32[1,128,4096]{2,1,0:T(8,128)} reshape(f32[128,4,8,128]{3,2,1,0:T(8,128)} %mul.380) | data formatting | bytes 4194304 | tf_op jit(solution)/shard_map/mul | solution.py:37
  118.9 2.7 %fusion.4 = f32[128]{0:T(128)S(1)} fusion(f32[2,64,4,8,128]{4,3,2,1,0:T(8,128)} %copy.271, f32[4096,128]{1,0:T(8,128)} %reshape.477, f32[4096]{0:T(1024)S(1)} %rsqrt.60), kind=kLoop, calls=%fused_computation.8 | loop fusion | flops 1572736 | bytes 4211200 | tf_op jit(solution)/shard_map/reduce_sum | solution.py:40
  121.7 1.2 fusion.22
  122.9 3.5 %subtract_convert_fusion = bf16[1,128,4096]{2,1,0:T(8,128)(2,1)} fusion(f32[1,128,4096]{2,1,0:T(8,128)} %mul.381, f32[1,128,4096]{2,1,0:T(8,128)S(1)} %copy-done.3, f32[1,128,4096]{2,1,0:T(8,128)S(1)} %copy-done.2, f32[1,128,4096]{2,1,0:T(8,128)S(1)} %copy-done.4, bf16[1,128,4096]{2,1,0:T(8,128)(2,1)S(1)} %copy-done.1, f32[4096]{0:T(1024)S(1)} %copy-done.27), kind=kLoop, calls=%fused_computation.15 | loop fusion | flops 3670016 | bytes 10502144 | tf_op jit(solution)/shard_map/convert_element_type | solution.py:113
  126.4 1.5 slice.109
  128.8 1.1 fusion.26
  130.6 110.8 %psum.7 = f32[2,128]{1,0:T(2,128)S(1)} all-reduce(f32[2,128]{1,0:T(2,128)S(1)} %pad_maximum_fusion.3), channel_id=1, replica_groups=mesh['dp'=64,'group'=8] {'dp','group'}, use_global_device_ids=true, to_apply=%region_16.17 | all-reduce | flops 256 | bytes 2048 | tf_op jit(solution)/shard_map/psum | solution.py:151
  (159 shorter events, 26.1 us)
Async XLA Ops:
  0.6 29.8 %copy-start.32 = (f32[128]{0:T(128)S(1)}, f32[128]{0:T(128)}, u32[]{:S(2)}) copy-start(f32[128]{0:T(128)} %param.15) | copy-start | bytes 1540
  0.6 31.1 %copy-start.1 = (bf16[1,128,4096]{2,1,0:T(8,128)(2,1)S(1)}, bf16[1,128,4096]{2,1,0:T(8,128)(2,1)}, u32[]{:S(2)}) copy-start(bf16[1,128,4096]{2,1,0:T(8,128)(2,1)} %param.10) | copy-start | bytes 3145732
  0.7 52.3 %collective-permute-start = (bf16[64,1024]{1,0:T(8,128)(2,1)}, bf16[64,1024]{1,0:T(8,128)(2,1)}, u32[]{:S(2)}, u32[]{:S(2)}) collective-permute-start(bf16[64,1024]{1,0:T(8,128)(2,1)} %bitcast.222), channel_id=1, source_target_pairs={{0,8},{8,16},{16,24},{24,32},{32,40},{40,48},{48,56},{56,64},{64,7... | collective-permute-start | bytes 393224 | tf_op jit(solution)/shard_map/ppermute | solution.py:27
  5.8 47.2 %collective-permute-start.1 = (bf16[64,1024]{1,0:T(8,128)(2,1)}, bf16[64,1024]{1,0:T(8,128)(2,1)}, u32[]{:S(2)}, u32[]{:S(2)}) collective-permute-start(bf16[64,1024]{1,0:T(8,128)(2,1)} %bitcast.223), channel_id=1, source_target_pairs={{0,16},{8,24},{16,32},{24,40},{32,48},{40,56},{48,64},{56,72},{64,... | collective-permute-start | bytes 393224 | tf_op jit(solution)/shard_map/ppermute | solution.py:27
  10.7 42.2 %collective-permute-start.2 = (bf16[64,1024]{1,0:T(8,128)(2,1)}, bf16[64,1024]{1,0:T(8,128)(2,1)}, u32[]{:S(2)}, u32[]{:S(2)}) collective-permute-start(bf16[64,1024]{1,0:T(8,128)(2,1)} %bitcast.224), channel_id=1, source_target_pairs={{0,24},{8,32},{16,40},{24,48},{32,56},{40,64},{48,72},{56,80},{64,... | collective-permute-start | bytes 393224 | tf_op jit(solution)/shard_map/ppermute | solution.py:27
  29.6 2.1 copy-start.7
  30.4 1.4 copy-start.30
  32.4 1.7 copy-start.42
  32.4 3.0 %copy-start.38 = (s32[1,2]{1,0:T(1,128)S(1)}, s32[1,2]{1,0:T(1,128)}, u32[]{:S(2)}) copy-start(s32[1,2]{1,0:T(1,128)} %param.16) | copy-start | bytes 28
  37.2 2.5 %copy-start.19 = (bf16[128,512]{0,1:T(8,128)(2,1)S(1)}, bf16[128,512]{0,1:T(8,128)(2,1)}, u32[]{:S(2)}) copy-start(bf16[128,512]{0,1:T(8,128)(2,1)} %get-tuple-element.52) | copy-start | bytes 393220
  44.9 2.8 %copy-start.11 = (f32[128,4,8]{2,1,0:T(4,128)S(1)}, f32[128,4,8]{2,1,0:T(4,128)}, u32[]{:S(2)}) copy-start(f32[128,4,8]{2,1,0:T(4,128)} %get-tuple-element.49) | copy-start | bytes 49156
  49.6 2.8 %copy-start.41 = (s32[2]{0:T(128)S(1)}, s32[2]{0:T(128)}, u32[]{:S(2)}) copy-start(s32[2]{0:T(128)} %fusion.39) | copy-start | bytes 28
  49.6 3.4 %copy-start.24 = (bf16[1,64,1024]{2,1,0:T(8,128)(2,1)S(1)}, bf16[1,64,1024]{2,1,0:T(8,128)(2,1)}, u32[]{:S(2)}) copy-start(bf16[1,64,1024]{2,1,0:T(8,128)(2,1)} %param.13) | copy-start | bytes 393220
  53.0 12.6 %copy-start.17 = (bf16[128,4,128]{2,0,1:T(8,128)(2,1)S(1)}, bf16[128,4,128]{2,0,1:T(8,128)(2,1)}, u32[]{:S(2)}) copy-start(bf16[128,4,128]{2,0,1:T(8,128)(2,1)} %multiply_convert_fusion) | copy-start | bytes 393220
  65.6 3.5 %copy-start.20 = (bf16[2,64,4,128]{3,1,2,0:T(8,128)(2,1)}, bf16[2,64,4,128]{3,1,2,0:T(8,128)(2,1)S(1)}, u32[]{:S(2)}) copy-start(bf16[2,64,4,128]{3,1,2,0:T(8,128)(2,1)S(1)} %fusion.24) | copy-start | bytes 393220
  65.7 3.5 %copy-start.12 = (bf16[2,128,4,128]{3,1,2,0:T(8,128)(2,1)}, bf16[2,128,4,128]{3,1,2,0:T(8,128)(2,1)S(1)}, u32[]{:S(2)}) copy-start(bf16[2,128,4,128]{3,1,2,0:T(8,128)(2,1)S(1)} %broadcast_in_dim.28) | copy-start | bytes 786436
  65.7 3.5 %copy-start.13 = (bf16[16,8,32,128]{3,2,1,0:T(8,128)(2,1)S(1)}, bf16[16,8,32,128]{3,2,1,0:T(8,128)(2,1)}, u32[]{:S(2)}) copy-start(bf16[16,8,32,128]{3,2,1,0:T(8,128)(2,1)} %copy.295) | copy-start | bytes 3145732
  65.7 3.5 %copy-start.28 = (pred[2,64,192]{2,1,0:T(8,128)(4,1)S(1)}, pred[2,64,192]{2,1,0:T(8,128)(4,1)}, u32[]{:S(2)}) copy-start(pred[2,64,192]{2,1,0:T(8,128)(4,1)} %fusion.32) | copy-start | bytes 73732
  69.2 3.0 %copy-start.18 = (bf16[128,4,128]{2,0,1:T(8,128)(2,1)S(1)}, bf16[128,4,128]{2,0,1:T(8,128)(2,1)}, u32[]{:S(2)}) copy-start(bf16[128,4,128]{2,0,1:T(8,128)(2,1)} %copy.256) | copy-start | bytes 393220
  73.9 1.8 copy-start.26
  73.9 1.8 copy-start.43
  75.7 2.2 copy-start.6
  75.7 3.0 %copy-start.8 = (f32[128,4,128]{2,0,1:T(8,128)S(1)}, f32[128,4,128]{2,0,1:T(8,128)}, u32[]{:S(2)}) copy-start(f32[128,4,128]{2,0,1:T(8,128)} %copy-done.7) | copy-start | bytes 786436
  75.7 3.0 %copy-start.33 = (f32[128]{0:T(128)S(1)}, f32[128]{0:T(128)}, u32[]{:S(2)}) copy-start(f32[128]{0:T(128)} %param.15) | copy-start | bytes 1540
  77.9 2.4 copy-start.21
  80.3 3.8 %copy-start.15 = (f32[2,192,4,128]{3,1,2,0:T(8,128)S(1)}, f32[2,192,4,128]{3,1,2,0:T(8,128)}, u32[]{:S(2)}) copy-start(f32[2,192,4,128]{3,1,2,0:T(8,128)} %convolution_bitcast_fusion.1) | copy-start | bytes 2359300
  84.9 2.6 %copy-start.40 = (f32[128]{0:T(128)S(1)}, f32[128]{0:T(128)}, u32[]{:S(2)}) copy-start(f32[128]{0:T(128)} %copy-done.39) | copy-start | bytes 1540
  86.1 1.3 copy-start
  89.0 2.8 %copy-start.14 = (f32[2,64,4,128]{3,1,2,0:T(8,128)S(1)}, f32[2,64,4,128]{3,1,2,0:T(8,128)}, u32[]{:S(2)}) copy-start(f32[2,64,4,128]{3,1,2,0:T(8,128)} %slice.107) | copy-start | bytes 786436
  97.5 10.2 %copy-start.36 = (f32[128,4]{0,1:T(4,128)S(1)}, f32[128,4]{0,1:T(4,128)}, u32[]{:S(2)}) copy-start(f32[128,4]{0,1:T(4,128)} %multiply_reduce_fusion.2) | copy-start | bytes 6148
  97.5 10.8 %copy-start.5 = (f32[2,64,4,8,128]{4,1,3,2,0:T(8,128)S(1)}, f32[2,64,4,8,128]{4,1,3,2,0:T(8,128)}, u32[]{:S(2)}) copy-start(f32[2,64,4,8,128]{4,1,3,2,0:T(8,128)} %get-tuple-element.68) | copy-start | bytes 6291460
  102.5 26.3 %collective-permute-start.3 = (bf16[64,1024]{1,0:T(8,128)(2,1)}, bf16[64,1024]{1,0:T(8,128)(2,1)}, u32[]{:S(2)}, u32[]{:S(2)}) collective-permute-start(bf16[64,1024]{1,0:T(8,128)(2,1)} %bitcast.204), channel_id=1, source_target_pairs={{8,0},{16,8},{24,16},{32,24},{40,32},{48,40},{56,48},{64,56},{72,6... | collective-permute-start | bytes 393224 | tf_op jit(solution)/shard_map/ppermute | solution.py:27
  104.5 24.3 %collective-permute-start.4 = (bf16[64,1024]{1,0:T(8,128)(2,1)}, bf16[64,1024]{1,0:T(8,128)(2,1)}, u32[]{:S(2)}, u32[]{:S(2)}) collective-permute-start(bf16[64,1024]{1,0:T(8,128)(2,1)} %bitcast.203), channel_id=1, source_target_pairs={{16,0},{24,8},{32,16},{40,24},{48,32},{56,40},{64,48},{72,56},{80,... | collective-permute-start | bytes 393224 | tf_op jit(solution)/shard_map/ppermute | solution.py:27
  106.5 22.3 %collective-permute-start.5 = (bf16[64,1024]{1,0:T(8,128)(2,1)}, bf16[64,1024]{1,0:T(8,128)(2,1)}, u32[]{:S(2)}, u32[]{:S(2)}) collective-permute-start(bf16[64,1024]{1,0:T(8,128)(2,1)} %bitcast.202), channel_id=1, source_target_pairs={{24,0},{32,8},{40,16},{48,24},{56,32},{64,40},{72,48},{80,56},{88,... | collective-permute-start | bytes 393224 | tf_op jit(solution)/shard_map/ppermute | solution.py:27
  116.0 5.7 %copy-start.10 = (bf16[1,128,1024]{1,2,0:T(8,128)(2,1)S(1)}, bf16[1,128,1024]{1,2,0:T(8,128)(2,1)}, u32[]{:S(2)}) copy-start(bf16[1,128,1024]{1,2,0:T(8,128)(2,1)} %copy-done.9) | copy-start | bytes 786436
  116.0 5.7 %copy-start.31 = (f32[128,4]{0,1:T(4,128)S(1)}, f32[128,4]{0,1:T(4,128)}, u32[]{:S(2)}) copy-start(f32[128,4]{0,1:T(4,128)} %copy-done.30) | copy-start | bytes 6148
  116.0 5.7 %copy-start.35 = (f32[128,4]{0,1:T(4,128)S(1)}, f32[128,4]{0,1:T(4,128)}, u32[]{:S(2)}) copy-start(f32[128,4]{0,1:T(4,128)} %get-tuple-element.58) | copy-start | bytes 6148
  116.0 5.7 %copy-start.37 = (f32[128,4]{0,1:T(4,128)S(1)}, f32[128,4]{0,1:T(4,128)}, u32[]{:S(2)}) copy-start(f32[128,4]{0,1:T(4,128)} %broadcast_multiply_fusion.3) | copy-start | bytes 6148
  116.0 6.9 %copy-start.4 = (f32[1,128,4096]{2,1,0:T(8,128)S(1)}, f32[1,128,4096]{2,1,0:T(8,128)}, u32[]{:S(2)}) copy-start(f32[1,128,4096]{2,1,0:T(8,128)} %reshape.465) | copy-start | bytes 6291460
  118.9 2.7 %copy-start.29 = (f32[512]{0:T(512)S(1)}, f32[512]{0:T(512)}, u32[]{:S(2)}) copy-start(f32[512]{0:T(512)} %broadcast_bitcast_fusion.1) | copy-start | bytes 6148
  118.9 3.9 %copy-start.2 = (f32[1,128,4096]{2,1,0:T(8,128)S(1)}, f32[1,128,4096]{2,1,0:T(8,128)}, u32[]{:S(2)}) copy-start(f32[1,128,4096]{2,1,0:T(8,128)} %mul.348) | copy-start | bytes 6291460
  118.9 3.9 %copy-start.3 = (f32[1,128,4096]{2,1,0:T(8,128)S(1)}, f32[1,128,4096]{2,1,0:T(8,128)}, u32[]{:S(2)}) copy-start(f32[1,128,4096]{2,1,0:T(8,128)} %mul.375) | copy-start | bytes 6291460
  118.9 4.0 %copy-start.27 = (f32[4096]{0:T(1024)S(1)}, f32[4096]{0:T(1024)}, u32[]{:S(2)}) copy-start(f32[4096]{0:T(1024)} %broadcast_bitcast_fusion) | copy-start | bytes 49156
  122.9 3.5 %copy-start.23 = (bf16[128,4,128]{0,2,1:T(8,128)(2,1)S(1)}, bf16[128,4,128]{0,2,1:T(8,128)(2,1)}, u32[]{:S(2)}) copy-start(bf16[128,4,128]{0,2,1:T(8,128)(2,1)} %copy.266) | copy-start | bytes 393220
  126.4 3.7 %copy-start.16 = (f32[64,4,128]{2,1,0:T(4,128)S(1)}, f32[64,4,128]{2,1,0:T(4,128)}, u32[]{:S(2)}) copy-start(f32[64,4,128]{2,1,0:T(4,128)} %reshape.467) | copy-start | bytes 393220
  126.4 3.7 %copy-start.34 = (f32[128]{0:T(128)S(1)}, f32[128]{0:T(128)}, u32[]{:S(2)}) copy-start(f32[128]{0:T(128)} %param.15) | copy-start | bytes 1540
  126.4 4.0 %copy-start.22 = (f32[256,128]{1,0:T(8,128)S(1)}, f32[256,128]{1,0:T(8,128)}, u32[]{:S(2)}) copy-start(f32[256,128]{1,0:T(8,128)} %reshape.471) | copy-start | bytes 393220
  126.4 115.9 %copy-start.25 = (bf16[1,64,1024]{2,1,0:T(8,128)(2,1)S(1)}, bf16[1,64,1024]{2,1,0:T(8,128)(2,1)}, u32[]{:S(2)}) copy-start(bf16[1,64,1024]{2,1,0:T(8,128)(2,1)} %param.13) | copy-start | bytes 393220
  (2 other events, 2.1 us)
where the time goes:
time: 244 us; the launch traced here: 243 us
  blocking collectives  111 us (45%)
  local copies, waits for them, and re-layouts  55.9 us (23%)
  other arithmetic  32.3 us (13%)
  starting transfers between devices  21.4 us (9%)
  matrix products  19.4 us (8%)
  between operations  3.31 us (1%)
    psum x1, blocking collectives, shards(): gain_total = lax.psum(gain_terms, ('dp', 'group'))  111 us
    ppermute x6, starting transfers between devices, from_behind(): return lax.ppermute(shard, axis, pairs)  21.4 us
    mul x6, local copies, waits for them, and re-layouts, norm_backward(): raw_rows * inverse ** 3  9.84 us
    unnamed x95, local copies, waits for them, and re-layouts  8.35 us
  transfers between devices with their start and end apart: 6, of which 0 were waited for; matrix products, arithmetic and copies ran while one was open for 23% of the time, Pallas kernels for 0%

commit v1 on v0

v1 whole, which is shorter than its diff:
```python
import functools
import math

import jax
import jax.numpy as jnp
from jax import lax
from jax.experimental import pallas as pl
from jax.experimental.pallas import tpu as pltpu
from jax.sharding import PartitionSpec as P

H = 32
KVH = 4
HD = 128
BLK = 64
SPAN = 4
P_SIZE = 64
QW = 4096
KW = 512
CT = 128
MEMBERS = H // KVH
ROWS = MEMBERS * BLK
NORM_EPS = 1e-06
SCALE = HD**-0.5
LOG2E = math.log2(math.e)
ZS = 16
YS = 4
GS = 8
F32 = jnp.float32
BF16 = jnp.bfloat16
MESH = pl.DeviceIdType.MESH


def nt(a, b):
    return lax.dot_general(a, b, (((1,), (1,)), ((), ())), preferred_element_type=F32)


def nn(a, b):
    return jnp.dot(a, b, preferred_element_type=F32)


def tn(a, b):
    return lax.dot_general(a, b, (((0,), (0,)), ((), ())), preferred_element_type=F32)


def fold8(a):
    return jnp.sum(a.reshape(a.shape[0] // 8, 8, a.shape[1]), axis=0)


def unit_factor(raw):
    return lax.rsqrt(jnp.mean(raw * raw, axis=-1, keepdims=True) + NORM_EPS)


def norm_backward(raw, inverse, weighted):
    return inverse * weighted - raw * (inverse * inverse * inverse) * jnp.mean(
        raw * weighted, axis=-1, keepdims=True
    )


def kernel(
    q_hbm, g_hbm, kv_hbm, p_hbm, qgain, kgain, owner, start,
    qg_hbm, kvg_hbm, pg_hbm, gains_ref,
    q_v, g_v, kv_v, p_v, qg_v, kvg_v, pg_v, cand, parts, gsend, grecv, ar1, ar2, ar3,
    q_sem, g_sem, kv_sem, p_sem, out_sem, f_send, f_recv, b_send, b_recv,
    a1_send, a1_recv, a2_send, a2_recv, a3_send, a3_recv,
):
    me = lax.axis_index("dp")
    grp = lax.axis_index("group")
    right, left = lax.rem(me + 1, ZS * YS), lax.rem(me + ZS * YS - 1, ZS * YS)
    my_y, my_z = me // ZS, lax.rem(me, ZS)

    def group_peer(j):
        return (me, lax.rem(grp + j, GS))

    def y_peer(j):
        return (lax.rem(my_y + j, YS) * ZS + my_z, grp)

    def z_peer(j):
        return (my_y * ZS + lax.rem(my_z + j, ZS), grp)

    p_load = pltpu.make_async_copy(p_hbm.at[0], p_v, p_sem)
    p_load.start()
    kv_load = pltpu.make_async_copy(kv_hbm.at[0], kv_v, kv_sem)
    kv_load.start()
    q_loads, g_loads = [], []
    for h in range(KVH):
        cols = pl.ds(h * MEMBERS * HD, MEMBERS * HD)
        q_loads.append(pltpu.make_async_copy(q_hbm.at[0, :, cols], q_v.at[:, cols], q_sem.at[h]))
        g_loads.append(pltpu.make_async_copy(g_hbm.at[0, :, cols], g_v.at[:, cols], g_sem.at[h]))
        q_loads[h].start()
        g_loads[h].start()

    barrier = pltpu.get_barrier_semaphore()
    partners = [(right, grp), (left, grp)]
    partners += [group_peer(j) for j in range(1, GS)]
    partners += [y_peer(j) for j in range(1, YS)]
    partners += [z_peer(j) for j in range(1, ZS)]
    for peer in partners:
        pl.semaphore_signal(barrier, inc=1, device_id=peer, device_id_type=MESH)
    pl.semaphore_wait(barrier, len(partners))

    def hop(k, h):
        copies = []
        for part in range(2):
            if k == 0:
                src = p_hbm.at[0, :, pl.ds(part * KW + h * HD, HD)]
            else:
                src = cand.at[k - 1, h, part]
            copies.append(
                pltpu.make_async_remote_copy(
                    src_ref=src,
                    dst_ref=cand.at[k, h, part],
                    send_sem=f_send.at[k, h, part],
                    recv_sem=f_recv.at[k, h, part],
                    device_id=(right, grp),
                    device_id_type=MESH,
                )
            )
        return copies

    def send(k, h):
        for copy in hop(k, h):
            copy.start()

    def arrive(k, h):
        for copy in hop(k, h):
            copy.wait_recv()

    def pump(k, h):
        arrive(k - 1, h)
        send(k, h)

    def back(k, h):
        return pltpu.make_async_remote_copy(
            src_ref=gsend.at[k, h],
            dst_ref=grecv.at[k, h],
            send_sem=b_send.at[k, h],
            recv_sem=b_recv.at[k, h],
            device_id=(left, grp),
            device_id_type=MESH,
        )

    def back_step(k, h):
        back(k + 1, h).wait_recv()
        gsend[k, h] = (parts[k + 1, h] + grecv[k + 1, h].astype(F32)).astype(BF16)
        back(k, h).start()

    send(0, 0)
    send(0, 1)

    cq = qgain[...]
    ck = kgain[...]
    cqk = cq * ck
    slot0 = me - owner[0, 0]
    slot1 = me - owner[0, 1]
    same = jnp.where((start[0, 1] == 1) | (owner[0, 0] != owner[0, 1]), 0.0, 1.0).astype(F32)
    key_at = lax.broadcasted_iota(jnp.int32, (BLK, ROWS), 0)
    row_at = lax.rem(lax.broadcasted_iota(jnp.int32, (BLK, ROWS), 1), BLK)
    tri = key_at <= row_at
    ones8 = jnp.ones((8, HD), BF16)
    sub16 = lax.broadcasted_iota(jnp.int32, (16, ROWS), 0)
    wide16 = jnp.concatenate(
        [jnp.zeros((16, HD), BF16), jnp.where(lax.broadcasted_iota(jnp.int32, (16, HD), 0) < 2, 1.0, 0.0).astype(BF16)],
        axis=1,
    )

    def rows_of(ref, n, h):
        return jnp.concatenate(
            [
                ref[n * BLK : (n + 1) * BLK, (h * MEMBERS + m) * HD : (h * MEMBERS + m + 1) * HD]
                for m in range(MEMBERS)
            ],
            axis=0,
        )

    def attend(n, h, keys, vals):
        count = keys.shape[0]
        x = rows_of(q_v, n, h)
        g = rows_of(g_v, n, h)
        s = lax.rsqrt(nt(ones8, x * x)[0:1] * (1.0 / HD) + NORM_EPS)
        raw = nt(keys, x)
        e = jnp.exp2(raw * (s * (SCALE * LOG2E)))
        if n == 0:
            e = jnp.concatenate([jnp.where(tri, e[:BLK], 0.0), e[BLK:]], axis=0)
        else:
            e = jnp.concatenate(
                [e[:BLK] * same, jnp.where(tri, e[BLK : 2 * BLK], 0.0), e[2 * BLK :]], axis=0
            )
        prob = e * (1.0 / jnp.sum(e, axis=0, keepdims=True))
        d_prob = nt(vals, g)
        delta = jnp.sum(prob * d_prob, axis=0, keepdims=True)
        d_score = prob * (d_prob - delta)
        m = jnp.sum(d_score * raw, axis=0, keepdims=True)
        d2 = (d_score * (s * SCALE)).astype(BF16)
        dk = nn(d2, x)
        dv = nn(prob.astype(BF16), g)
        fac = s * s * s * m * (SCALE / HD)
        hi = fac.astype(BF16).astype(F32)
        lo = fac - hi
        extra = jnp.where(sub16 == 0, hi, jnp.where(sub16 == 1, lo, 0.0)).astype(BF16)
        lhs = jnp.concatenate([d2, extra], axis=0)
        rhs = jnp.concatenate(
            [jnp.concatenate([keys, jnp.zeros((count, HD), BF16)], axis=1), wide16], axis=0
        )
        z = tn(lhs, rhs)
        dx = (z[:, :HD] - x.astype(F32) * z[:, HD:]).astype(BF16)
        for mm in range(MEMBERS):
            c = (h * MEMBERS + mm) * HD
            qg_v[n * BLK : (n + 1) * BLK, c : c + HD] = dx[mm * BLK : (mm + 1) * BLK]
        return dk, dv

    p_load.wait()
    kv_load.wait()

    def pick(slot, h, part):
        c = part * KW + h * HD
        own = p_v[:, c : c + HD].astype(F32)
        got = [cand[k, h, part].astype(F32) for k in range(SPAN - 1)]
        return jnp.where(
            slot == 0, own, jnp.where(slot == 1, got[0], jnp.where(slot == 2, got[1], got[2]))
        )

    def head(h, between):
        q_loads[h].wait()
        g_loads[h].wait()
        k_raw = kv_v[:, h * HD : (h + 1) * HD].astype(F32)
        k_inv = unit_factor(k_raw)
        k_full = k_raw * k_inv * cqk
        k_b = k_full.astype(BF16)
        v_b = kv_v[:, KW + h * HD : KW + (h + 1) * HD]
        p_full, p_b, w_b = [], [], []
        for slot in (slot0, slot1):
            praw = pick(slot, h, 0)
            full = praw * unit_factor(praw) * cqk
            p_full.append(full)
            p_b.append(full.astype(BF16))
            w_b.append(pick(slot, h, 1).astype(BF16))
        dk0, dv0 = attend(
            0, h, jnp.concatenate([k_b[:BLK], p_b[0]], axis=0), jnp.concatenate([v_b[:BLK], w_b[0]], axis=0)
        )
        between()
        dk1, dv1 = attend(1, h, jnp.concatenate([k_b, p_b[1]], axis=0), jnp.concatenate([v_b, w_b[1]], axis=0))
        d_p = [(cq * dk0[BLK:], dv0[BLK:]), (cq * dk1[2 * BLK :], dv1[2 * BLK :])]
        for part in range(2):
            for k in range(SPAN):
                term = jnp.where(slot0 == k, d_p[0][part], 0.0) + jnp.where(slot1 == k, d_p[1][part], 0.0)
                if k == SPAN - 1:
                    gsend[k - 1, h, part] = term.astype(BF16)
                else:
                    parts[k, h, part] = term
        back(SPAN - 2, h).start()
        dk = jnp.concatenate([dk0[:BLK] + dk1[:BLK], dk1[BLK : 2 * BLK]], axis=0)
        dv = jnp.concatenate([dv0[:BLK] + dv1[:BLK], dv1[BLK : 2 * BLK]], axis=0)
        kvg_v[:, h * HD : (h + 1) * HD] = norm_backward(k_raw, k_inv, cqk * dk).astype(BF16)
        kvg_v[:, KW + h * HD : KW + (h + 1) * HD] = dv.astype(BF16)
        return fold8(k_full * dk) + fold8(p_full[0] * dk0[BLK:]) + fold8(p_full[1] * dk1[2 * BLK :])

    def q_out(h):
        cols = pl.ds(h * MEMBERS * HD, MEMBERS * HD)
        return pltpu.make_async_copy(qg_v.at[:, cols], qg_hbm.at[0, :, cols], out_sem.at[h])

    pump(1, 0)
    send(0, 2)
    pump(1, 1)
    pump(2, 0)
    send(0, 3)
    pump(1, 2)
    arrive(2, 0)

    def between0():
        pump(2, 1)

    total = head(0, between0)
    q_out(0).start()
    pump(1, 3)
    pump(2, 2)
    arrive(2, 1)

    def between1():
        pump(2, 3)
        back_step(1, 0)

    total += head(1, between1)
    q_out(1).start()
    arrive(2, 2)
    back_step(0, 0)

    def between2():
        back_step(1, 1)

    total += head(2, between2)
    q_out(2).start()
    arrive(2, 3)
    back_step(0, 1)

    def between3():
        back_step(1, 2)

    total += head(3, between3)
    q_out(3).start()
    kv_out = pltpu.make_async_copy(kvg_v, kvg_hbm.at[0], out_sem.at[KVH])
    kv_out.start()

    def exchange(buf, mine, size, peer_of, send_sem, recv_sem):
        def copy(j):
            return pltpu.make_async_remote_copy(
                src_ref=buf.at[mine],
                dst_ref=buf.at[mine],
                send_sem=send_sem.at[j],
                recv_sem=recv_sem.at[mine],
                device_id=peer_of(j),
                device_id_type=MESH,
            )

        def start_all():
            for j in range(1, size):
                copy(j).start()

        def finish():
            for j in range(1, size):
                other = lax.rem(mine + j, size)
                pltpu.make_async_remote_copy(
                    src_ref=buf.at[other],
                    dst_ref=buf.at[other],
                    send_sem=send_sem.at[j],
                    recv_sem=recv_sem.at[other],
                    device_id=peer_of(j),
                    device_id_type=MESH,
                ).wait_recv()
            return jnp.sum(buf[...], axis=0)

        def drain():
            for j in range(1, size):
                copy(j).wait_send()

        return start_all, finish, drain

    go1, end1, drain1 = exchange(ar1, grp, GS, group_peer, a1_send, a1_recv)
    go2, end2, drain2 = exchange(ar2, my_y, YS, y_peer, a2_send, a2_recv)
    go3, end3, drain3 = exchange(ar3, my_z, ZS, z_peer, a3_send, a3_recv)

    ar1[grp] = total
    go1()
    back_step(0, 2)
    back_step(1, 3)

    def finish_prompt(h):
        back(0, h).wait_recv()
        both = parts[0, h] + grecv[0, h].astype(F32)
        raw = p_v[:, h * HD : (h + 1) * HD].astype(F32)
        pg_v[:, h * HD : (h + 1) * HD] = norm_backward(raw, unit_factor(raw), ck * both[0]).astype(BF16)
        pg_v[:, KW + h * HD : KW + (h + 1) * HD] = both[1].astype(BF16)

    finish_prompt(0)
    finish_prompt(1)
    ar2[my_y] = end1()
    go2()
    back_step(0, 3)
    finish_prompt(2)
    ar3[my_z] = end2()
    go3()
    finish_prompt(3)
    p_out = pltpu.make_async_copy(pg_v, pg_hbm.at[0], out_sem.at[KVH + 1])
    p_out.start()
    summed = jnp.sum(end3(), axis=0, keepdims=True) * (1.0 / math.sqrt(GS * ZS * YS * CT))
    gains_ref[0:1] = summed / cq
    gains_ref[1:2] = summed / ck

    for k in range(SPAN - 1):
        for h in range(KVH):
            for copy in hop(k, h):
                copy.wait_send()
            back(k, h).wait_send()
    drain1()
    drain2()
    drain3()
    for h in range(KVH):
        q_out(h).wait()
    kv_out.wait()
    p_out.wait()


def shards(queries, out_grad, keys_values, prompt_kv, q_gain, k_gain, block_owner, block_start):
    anywhere = pl.BlockSpec(memory_space=pl.ANY)
    vmem = pl.BlockSpec(memory_space=pltpu.VMEM)
    smem = pl.BlockSpec(memory_space=pltpu.SMEM)
    dma = pltpu.SemaphoreType.DMA
    return pl.pallas_call(
        kernel,
        out_shape=(
            jax.ShapeDtypeStruct((1, CT, QW), BF16),
            jax.ShapeDtypeStruct((1, CT, 2 * KW), BF16),
            jax.ShapeDtypeStruct((1, P_SIZE, 2 * KW), BF16),
            jax.ShapeDtypeStruct((2, HD), F32),
        ),
        in_specs=[anywhere] * 4 + [vmem] * 2 + [smem] * 2,
        out_specs=(anywhere, anywhere, anywhere, vmem),
        scratch_shapes=[
            pltpu.VMEM((CT, QW), BF16),
            pltpu.VMEM((CT, QW), BF16),
            pltpu.VMEM((CT, 2 * KW), BF16),
            pltpu.VMEM((P_SIZE, 2 * KW), BF16),
            pltpu.VMEM((CT, QW), BF16),
            pltpu.VMEM((CT, 2 * KW), BF16),
            pltpu.VMEM((P_SIZE, 2 * KW), BF16),
            pltpu.VMEM((SPAN - 1, KVH, 2, P_SIZE, HD), BF16),
            pltpu.VMEM((SPAN - 1, KVH, 2, P_SIZE, HD), F32),
            pltpu.VMEM((SPAN - 1, KVH, 2, P_SIZE, HD), BF16),
            pltpu.VMEM((SPAN - 1, KVH, 2, P_SIZE, HD), BF16),
            pltpu.VMEM((GS, 8, HD), F32),
            pltpu.VMEM((YS, 8, HD), F32),
            pltpu.VMEM((ZS, 8, HD), F32),
            dma((KVH,)),
            dma((KVH,)),
            dma,
            dma,
            dma((KVH + 2,)),
            dma((SPAN - 1, KVH, 2)),
            dma((SPAN - 1, KVH, 2)),
            dma((SPAN - 1, KVH)),
            dma((SPAN - 1, KVH)),
            dma((GS,)),
            dma((GS,)),
            dma((YS,)),
            dma((YS,)),
            dma((ZS,)),
            dma((ZS,)),
        ],
        compiler_params=pltpu.CompilerParams(
            collective_id=0, has_side_effects=True, vmem_limit_bytes=48 * 1024 * 1024
        ),
        name="prefix_attention_grad",
    )(
        queries,
        out_grad,
        keys_values,
        prompt_kv,
        q_gain.reshape(1, HD),
        k_gain.reshape(1, HD),
        block_owner,
        block_start,
    )


def solution(mesh):
    placed = (
        P("group", "dp", None),
        P("group", "dp", None),
        P("group", "dp", None),
        P("group", "dp", None),
        P(),
        P(),
        P("group", "dp"),
        P("group", "dp"),
    )
    return jax.shard_map(
        shards,
        mesh=mesh,
        in_specs=placed,
        out_specs=(P("group", "dp", None), P("group", "dp", None), P("group", "dp", None), P()),
        check_vma=False,
    )
```

time: 244 us -> 64.4 us (0.26)
  blocking collectives: 111 us -> 0 us
  Pallas kernels: 0 us -> 55.6 us
  local copies, waits for them, and re-layouts: 55.9 us -> 7.86 us
  other arithmetic: 32.3 us -> 0 us
  starting transfers between devices: 21.4 us -> 0 us
  matrix products: 19.4 us -> 0 us
  between operations: 3.31 us -> 0.68 us
    psum x1 -> x0, blocking collectives: 111 us -> none  [shards(): gain_total = lax.psum(gain_terms, ('dp', 'group'))]
    pallas_call x0 -> x1, Pallas kernels: none -> 55.6 us  [shards(): pl.pallas_call(kernel, out_shape=(jax.ShapeDtypeStruct((1, CT, QW), BF16)...]
    ppermute x6 -> x0, starting transfers between devices: 21.4 us -> none  [from_behind(): return lax.ppermute(shard, axis, pairs)]
    dot_general x7 -> x0, matrix products: 19.4 us -> none  [the longest x1 3.82 us: attention_terms(): jnp.einsum('nkgbs,nskd->nbkgd', d_score, key_all, preferred_element_type=...]
    mul x12 -> x0, local copies, waits for them, and re-layouts: 18.4 us -> none  [the longest x6 9.84 us: norm_backward(): raw_rows * inverse ** 3]
    reshape x12 -> x0, local copies, waits for them, and re-layouts: 12.7 us -> none  [the longest x2 3.67 us: attention_terms(): d_pvalues.reshape(NB, P_SIZE, KW)]
    reduce_sum x12 -> x0, other arithmetic: 10 us -> none  [the longest x4 3.99 us: norm_backward(): jnp.sum((raw_rows * inverse * upstream).reshape(-1, raw_rows.shape[-1]),...]
    convert_element_type x5 -> x0, other arithmetic: 6.65 us -> none  [the longest x1 3.48 us: attention_terms(): query_grad = d_query.reshape(CT, QW).astype(jnp.bfloat16)]
  transfers between devices with their start and end apart: 6 -> 0, of which waited for: 0 -> 0; matrix products, arithmetic and copies ran while one was open for 23% -> 0% of each run, Pallas kernels for 0% -> 0%
where the time goes in v1:
time: 64.4 us; the launch traced here: 64.2 us
  Pallas kernels  55.6 us (86%)
  local copies, waits for them, and re-layouts  7.86 us (12%)
  between operations  0.68 us (1%)
    pallas_call x1, Pallas kernels, shards(): pl.pallas_call(kernel, out_shape=(jax.ShapeDtypeStruct((1, CT, QW), BF16)...  55.6 us
    unnamed x20, local copies, waits for them, and re-layouts  7.86 us

profile of v1, /device:TPU:1, one launch (start us, length us, event | category | flops | bytes accessed | tf_op | source)
XLA Modules:
  0.0 64.2 jit_solution(6622963211355729555)
XLA Ops:
  0.6 0.0 copy-start.7
  0.6 0.0 copy-start.4
  0.7 0.0 copy-start.5
  0.7 0.0 copy-start.6
  0.7 0.6 copy-done.7
  1.3 0.0 copy-done.4
  1.3 0.0 copy-done.5
  1.3 0.0 copy-done.6
  1.3 0.0 copy-start
  1.3 1.2 %copy-done = bf16[1,128,4096]{2,1,0:T(8,128)(2,1)S(1)} copy-done((bf16[1,128,4096]{2,1,0:T(8,128)(2,1)S(1)}, bf16[1,128,4096]{2,1,0:T(8,128)(2,1)}, u32[]{:S(2)}) %copy-start) | copy-done | bytes 1048600
  2.6 0.0 copy-start.1
  2.6 1.2 %copy-done.1 = bf16[1,128,4096]{2,1,0:T(8,128)(2,1)S(1)} copy-done((bf16[1,128,4096]{2,1,0:T(8,128)(2,1)S(1)}, bf16[1,128,4096]{2,1,0:T(8,128)(2,1)}, u32[]{:S(2)}) %copy-start.1) | copy-done | bytes 1048600
  3.8 0.0 copy-start.2
  3.8 0.9 %copy-done.2 = bf16[1,128,1024]{2,1,0:T(8,128)(2,1)S(1)} copy-done((bf16[1,128,1024]{2,1,0:T(8,128)(2,1)S(1)}, bf16[1,128,1024]{2,1,0:T(8,128)(2,1)}, u32[]{:S(2)}) %copy-start.2) | copy-done | bytes 262168
  4.7 0.0 copy-start.3
  4.7 0.9 %copy-done.3 = bf16[1,64,1024]{2,1,0:T(8,128)(2,1)S(1)} copy-done((bf16[1,64,1024]{2,1,0:T(8,128)(2,1)S(1)}, bf16[1,64,1024]{2,1,0:T(8,128)(2,1)}, u32[]{:S(2)}) %copy-start.3) | copy-done | bytes 131096
  5.6 55.6 %prefix_attention_grad.1 = (bf16[1,128,4096]{2,1,0:T(8,128)(2,1)S(1)}, bf16[1,128,1024]{2,1,0:T(8,128)(2,1)S(1)}, bf16[1,64,1024]{2,1,0:T(8,128)(2,1)S(1)}, f32[2,128]{1,0:T(2,128)S(1)}) custom-call(bf16[1,128,4096]{2,1,0:T(8,128)(2,1)S(1)} %copy-done, bf16[1,128,4096]{2,1,0:T(8,128)(2,1)S(1)} %copy-done.1, bf16[1,128,1024]{2,1,0:T(8,128)(2,1)S(1)} %copy-done.2, ...), custom_call_target="tpu_custom_call" | custom-call | tf_op jit(solution)/shard_map/prefix_attention_grad/pallas_call | solution.py:387
  61.3 1.0 %copy.16 = bf16[1,128,4096]{2,1,0:T(8,128)(2,1)} copy(bf16[1,128,4096]{2,1,0:T(8,128)(2,1)S(1)} %get-tuple-element.8) | data formatting | bytes 2097152
  62.3 0.7 %copy.17 = bf16[1,128,1024]{2,1,0:T(8,128)(2,1)} copy(bf16[1,128,1024]{2,1,0:T(8,128)(2,1)S(1)} %get-tuple-element.9) | data formatting | bytes 524288
  63.0 0.7 %copy.18 = bf16[1,64,1024]{2,1,0:T(8,128)(2,1)} copy(bf16[1,64,1024]{2,1,0:T(8,128)(2,1)S(1)} %get-tuple-element.10) | data formatting | bytes 262144
  63.6 0.6 copy.19
Async XLA Ops:
  0.6 0.7 %copy-start.7 = (s32[1,2]{1,0:T(1,128)S(1)}, s32[1,2]{1,0:T(1,128)}, u32[]{:S(2)}) copy-start(s32[1,2]{1,0:T(1,128)} %start.1) | copy-start | bytes 28
  0.6 0.7 %copy-start.4 = (f32[128]{0:T(128)S(1)}, f32[128]{0:T(128)}, u32[]{:S(2)}) copy-start(f32[128]{0:T(128)} %param.12) | copy-start | bytes 1540
  0.7 0.7 %copy-start.5 = (f32[128]{0:T(128)S(1)}, f32[128]{0:T(128)}, u32[]{:S(2)}) copy-start(f32[128]{0:T(128)} %param.13) | copy-start | bytes 1540
  0.7 0.7 %copy-start.6 = (s32[1,2]{1,0:T(1,128)S(1)}, s32[1,2]{1,0:T(1,128)}, u32[]{:S(2)}) copy-start(s32[1,2]{1,0:T(1,128)} %owner.1) | copy-start | bytes 28
  1.3 1.2 %copy-start = (bf16[1,128,4096]{2,1,0:T(8,128)(2,1)S(1)}, bf16[1,128,4096]{2,1,0:T(8,128)(2,1)}, u32[]{:S(2)}) copy-start(bf16[1,128,4096]{2,1,0:T(8,128)(2,1)} %q_hbm.1) | copy-start | bytes 3145732
  2.6 1.2 %copy-start.1 = (bf16[1,128,4096]{2,1,0:T(8,128)(2,1)S(1)}, bf16[1,128,4096]{2,1,0:T(8,128)(2,1)}, u32[]{:S(2)}) copy-start(bf16[1,128,4096]{2,1,0:T(8,128)(2,1)} %g_hbm.1) | copy-start | bytes 3145732
  3.8 0.9 %copy-start.2 = (bf16[1,128,1024]{2,1,0:T(8,128)(2,1)S(1)}, bf16[1,128,1024]{2,1,0:T(8,128)(2,1)}, u32[]{:S(2)}) copy-start(bf16[1,128,1024]{2,1,0:T(8,128)(2,1)} %kv_hbm.1) | copy-start | bytes 786436
  4.7 0.9 %copy-start.3 = (bf16[1,64,1024]{2,1,0:T(8,128)(2,1)S(1)}, bf16[1,64,1024]{2,1,0:T(8,128)(2,1)}, u32[]{:S(2)}) copy-start(bf16[1,64,1024]{2,1,0:T(8,128)(2,1)} %p_hbm.1) | copy-start | bytes 393220

commit v2 on v1

v2 whole, which is shorter than its diff:
```python
import functools
import math

import jax
import jax.numpy as jnp
from jax import lax
from jax.experimental import pallas as pl
from jax.experimental.pallas import tpu as pltpu
from jax.sharding import PartitionSpec as P

H = 32
KVH = 4
HD = 128
BLK = 64
SPAN = 4
P_SIZE = 64
QW = 4096
KW = 512
CT = 128
MEMBERS = H // KVH
ROWS = MEMBERS * BLK
NORM_EPS = 1e-06
SCALE = HD**-0.5
LOG2E = math.log2(math.e)
ZS = 16
YS = 4
GS = 8
F32 = jnp.float32
BF16 = jnp.bfloat16
MESH = pl.DeviceIdType.MESH


def nt(a, b):
    return lax.dot_general(a, b, (((1,), (1,)), ((), ())), preferred_element_type=F32)


def nn(a, b):
    return jnp.dot(a, b, preferred_element_type=F32)


def tn(a, b):
    return lax.dot_general(a, b, (((0,), (0,)), ((), ())), preferred_element_type=F32)


def fold8(a):
    return jnp.sum(a.reshape(a.shape[0] // 8, 8, a.shape[1]), axis=0)


def unit_factor(raw):
    return lax.rsqrt(jnp.mean(raw * raw, axis=-1, keepdims=True) + NORM_EPS)


def norm_backward(raw, inverse, weighted):
    return inverse * weighted - raw * (inverse * inverse * inverse) * jnp.mean(
        raw * weighted, axis=-1, keepdims=True
    )


def kernel(
    q_hbm, g_hbm, kv_hbm, p_hbm, qgain_hbm, kgain_hbm, owner_hbm, start_hbm,
    qg_hbm, kvg_hbm, pg_hbm, gains_ref,
    q_v, g_v, kv_v, p_v, qgain, kgain, owner, start, qg_v, kvg_v, pg_v,
    e_v, d_v, lhs_v, cand, parts, gsend, grecv, ar1, ar2,
    q_sem, g_sem, small_sem, out_sem, f_send, f_recv, b_send, b_recv,
    a1_send, a1_recv, a2_send, a2_recv,
):
    me = lax.axis_index("dp")
    grp = lax.axis_index("group")
    right, left = lax.rem(me + 1, ZS * YS), lax.rem(me + ZS * YS - 1, ZS * YS)
    my_y, my_z = me // ZS, lax.rem(me, ZS)

    def plane_at(j):
        return lax.rem(my_y + j // GS, YS), lax.rem(grp + j % GS, GS)

    def plane_peer(j):
        y, g = plane_at(j)
        return (y * ZS + my_z, g)

    def plane_slot(j):
        y, g = plane_at(j)
        return y * GS + g

    def z_peer(j):
        return (my_y * ZS + lax.rem(my_z + j, ZS), grp)

    def z_slot(j):
        return lax.rem(my_z + j, ZS)

    def ring_steps(j, size):
        return min(j, size - j)

    plane_order = sorted(
        range(1, YS * GS),
        key=lambda j: -ring_steps(j // GS, YS) - ring_steps((j % GS + 1) // 2, GS // 2),
    )
    z_order = sorted(range(1, ZS), key=lambda j: -ring_steps(j, ZS))

    barrier = pltpu.get_barrier_semaphore()
    partners = [(right, grp), (left, grp)]
    partners += [z_peer(j) for j in z_order]
    partners += [plane_peer(j) for j in plane_order]
    for peer in partners:
        pl.semaphore_signal(barrier, inc=1, device_id=peer, device_id_type=MESH)

    small = [
        pltpu.make_async_copy(src, dst, small_sem.at[i])
        for i, (src, dst) in enumerate(
            [
                (kv_hbm.at[0], kv_v),
                (qgain_hbm, qgain),
                (kgain_hbm, kgain),
                (owner_hbm, owner),
                (start_hbm, start),
                (p_hbm.at[0], p_v),
            ]
        )
    ]
    q_loads, g_loads = [], []
    for h in range(KVH):
        cols = pl.ds(h * MEMBERS * HD, MEMBERS * HD)
        q_loads.append(pltpu.make_async_copy(q_hbm.at[0, :, cols], q_v.at[:, cols], q_sem.at[h]))
        g_loads.append(pltpu.make_async_copy(g_hbm.at[0, :, cols], g_v.at[:, cols], g_sem.at[h]))
    for load in small[:3] + [q_loads[0], g_loads[0]] + small[3:] + q_loads[1:] + g_loads[1:]:
        load.start()

    def hop(k, h):
        copies = []
        for part in range(2):
            if k == 0:
                src = p_hbm.at[0, :, pl.ds(part * KW + h * HD, HD)]
            else:
                src = cand.at[k - 1, h, part]
            copies.append(
                pltpu.make_async_remote_copy(
                    src_ref=src,
                    dst_ref=cand.at[k, h, part],
                    send_sem=f_send.at[k, h, part],
                    recv_sem=f_recv.at[k, h, part],
                    device_id=(right, grp),
                    device_id_type=MESH,
                )
            )
        return copies

    def send(k, h):
        for copy in hop(k, h):
            copy.start()

    def arrive(k, h):
        for copy in hop(k, h):
            copy.wait_recv()

    def pump(k, h):
        arrive(k - 1, h)
        send(k, h)

    def back(k, h):
        return pltpu.make_async_remote_copy(
            src_ref=gsend.at[k, h],
            dst_ref=grecv.at[k, h],
            send_sem=b_send.at[k, h],
            recv_sem=b_recv.at[k, h],
            device_id=(left, grp),
            device_id_type=MESH,
        )

    def back_step(k, h):
        back(k + 1, h).wait_recv()
        gsend[k, h] = (parts[k + 1, h] + grecv[k + 1, h].astype(F32)).astype(BF16)
        back(k, h).start()

    def exchange(buf, mine, order, peer_of, slot_of, send_sem, recv_sem):
        def copy(j, slot):
            return pltpu.make_async_remote_copy(
                src_ref=buf.at[slot],
                dst_ref=buf.at[slot],
                send_sem=send_sem.at[j],
                recv_sem=recv_sem.at[slot],
                device_id=peer_of(j),
                device_id_type=MESH,
            )

        def go(value):
            buf[mine] = value
            for j in order:
                copy(j, mine).start()

        def finish():
            for j in reversed(order):
                copy(j, slot_of(j)).wait_recv()
            return jnp.sum(buf[...], axis=0)

        def drain():
            for j in order:
                copy(j, mine).wait_send()

        return go, finish, drain

    go1, end1, drain1 = exchange(
        ar1, my_y * GS + grp, plane_order, plane_peer, plane_slot, a1_send, a1_recv
    )
    go2, end2, drain2 = exchange(ar2, my_z, z_order, z_peer, z_slot, a2_send, a2_recv)

    pl.semaphore_wait(barrier, len(partners))
    for h in range(KVH):
        send(0, h)

    key_at = lax.broadcasted_iota(jnp.int32, (BLK, ROWS), 0)
    row_at = lax.rem(lax.broadcasted_iota(jnp.int32, (BLK, ROWS), 1), BLK)
    tri = key_at <= row_at
    ones8 = jnp.ones((8, HD), BF16)
    sub16 = lax.broadcasted_iota(jnp.int32, (16, ROWS), 0)
    wide16 = jnp.concatenate(
        [
            jnp.zeros((16, HD), BF16),
            jnp.where(lax.broadcasted_iota(jnp.int32, (16, HD), 0) < 2, 1.0, 0.0).astype(BF16),
        ],
        axis=1,
    )
    for load in small:
        load.wait()
    cq = qgain[...]
    ck = kgain[...]
    cqk = cq * ck
    slots = (me - owner[0, 0], me - owner[0, 1])
    same = jnp.where((start[0, 1] == 1) | (owner[0, 0] != owner[0, 1]), 0.0, 1.0).astype(F32)

    def rows_of(ref, n, h):
        return jnp.concatenate(
            [
                ref[n * BLK : (n + 1) * BLK, (h * MEMBERS + m) * HD : (h * MEMBERS + m + 1) * HD]
                for m in range(MEMBERS)
            ],
            axis=0,
        )

    def local_keys(h):
        raw = kv_v[:, h * HD : (h + 1) * HD].astype(F32)
        inverse = unit_factor(raw)
        return raw, inverse, raw * inverse * cqk

    def over_keys(a):
        return jnp.sum(a, axis=0, keepdims=True)

    stats = {}

    def before(h):
        q_loads[h].wait()
        g_loads[h].wait()
        k_b = local_keys(h)[2].astype(BF16)
        v_b = kv_v[:, KW + h * HD : KW + (h + 1) * HD]
        for n in range(2):
            count = (n + 1) * BLK
            at = n * BLK
            x = rows_of(q_v, n, h)
            g = rows_of(g_v, n, h)
            s = lax.rsqrt(nt(ones8, x * x)[0:1] * (1.0 / HD) + NORM_EPS)
            raw = nt(k_b[:count], x)
            e = jnp.exp2(raw * (s * (SCALE * LOG2E)))
            if n == 0:
                e = jnp.where(tri, e, 0.0)
            else:
                e = jnp.concatenate([e[:BLK] * same, jnp.where(tri, e[BLK:], 0.0)], axis=0)
            d = nt(v_b[:count], g)
            e_v[h, at : at + count] = e
            d_v[h, at : at + count] = d
            er = e * raw
            stats[h, n] = (s, over_keys(e), over_keys(e * d), over_keys(er), over_keys(er * d))

    def pick(slot, h, part):
        c = part * KW + h * HD
        own = p_v[:, c : c + HD].astype(F32)
        got = [cand[k, h, part].astype(F32) for k in range(SPAN - 1)]
        return jnp.where(
            slot == 0, own, jnp.where(slot == 1, got[0], jnp.where(slot == 2, got[1], got[2]))
        )

    kept = {}

    def middle(h):
        arrive(SPAN - 2, h)
        full_l = local_keys(h)[2]
        k_b = full_l.astype(BF16)
        d_p, dks, dvs = [], [], []
        total = jnp.zeros((8, HD), F32)
        for n in range(2):
            count = (n + 1) * BLK
            at = n * BLK
            praw = pick(slots[n], h, 0)
            full = praw * unit_factor(praw) * cqk
            p_b = full.astype(BF16)
            w_b = pick(slots[n], h, 1).astype(BF16)
            x = rows_of(q_v, n, h)
            g = rows_of(g_v, n, h)
            s, t, u, xs, ws = stats[h, n]
            raw = nt(p_b, x)
            e_p = jnp.exp2(raw * (s * (SCALE * LOG2E)))
            d_prob = nt(w_b, g)
            inv = 1.0 / (t + over_keys(e_p))
            e_d = e_p * d_prob
            er = e_p * raw
            delta = (u + over_keys(e_d)) * inv
            m = (ws + over_keys(er * d_prob) - delta * (xs + over_keys(er))) * inv
            r = s * SCALE
            prob_l = e_v[h, at : at + count] * inv
            prob_p = e_p * inv
            d2 = jnp.concatenate(
                [
                    (prob_l * ((d_v[h, at : at + count] - delta) * r)).astype(BF16),
                    (prob_p * ((d_prob - delta) * r)).astype(BF16),
                ],
                axis=0,
            )
            prob = jnp.concatenate([prob_l.astype(BF16), prob_p.astype(BF16)], axis=0)
            dk = nn(d2, x)
            dv = nn(prob, g)
            fac = s * s * s * m * (SCALE / HD)
            hi = fac.astype(BF16).astype(F32)
            extra = jnp.where(sub16 == 0, hi, jnp.where(sub16 == 1, fac - hi, 0.0)).astype(BF16)
            lhs_v[h, n, : count + BLK] = d2
            lhs_v[h, n, count + BLK : count + BLK + 16] = extra
            kept[h, n] = jnp.concatenate([k_b[:count], p_b], axis=0)
            d_p.append((cq * dk[count:], dv[count:]))
            dks.append(dk[:count])
            dvs.append(dv[:count])
            total += fold8(full * dk[count:])
        for part in range(2):
            for k in range(SPAN):
                term = jnp.where(slots[0] == k, d_p[0][part], 0.0) + jnp.where(
                    slots[1] == k, d_p[1][part], 0.0
                )
                if k == SPAN - 1:
                    gsend[k - 1, h, part] = term.astype(BF16)
                else:
                    parts[k, h, part] = term
        back(SPAN - 2, h).start()
        dk = jnp.concatenate([dks[0] + dks[1][:BLK], dks[1][BLK:]], axis=0)
        dv = jnp.concatenate([dvs[0] + dvs[1][:BLK], dvs[1][BLK:]], axis=0)
        kvg_v[:, KW + h * HD : KW + (h + 1) * HD] = dv.astype(BF16)
        kept[h] = dk
        return total + fold8(full_l * dk)

    def q_out(h):
        cols = pl.ds(h * MEMBERS * HD, MEMBERS * HD)
        return pltpu.make_async_copy(qg_v.at[:, cols], qg_hbm.at[0, :, cols], out_sem.at[h])

    def after(h):
        raw_l, inverse, _ = local_keys(h)
        kvg_v[:, h * HD : (h + 1) * HD] = norm_backward(raw_l, inverse, cqk * kept[h]).astype(BF16)
        for n in range(2):
            count = (n + 2) * BLK
            rhs = jnp.concatenate(
                [jnp.concatenate([kept[h, n], jnp.zeros((count, HD), BF16)], axis=1), wide16], axis=0
            )
            z = tn(lhs_v[h, n, : count + 16], rhs)
            x = rows_of(q_v, n, h).astype(F32)
            dx = (z[:, :HD] - x * z[:, HD:]).astype(BF16)
            for m in range(MEMBERS):
                c = (h * MEMBERS + m) * HD
                qg_v[n * BLK : (n + 1) * BLK, c : c + HD] = dx[m * BLK : (m + 1) * BLK]
        q_out(h).start()

    for h in range(KVH - 1):
        before(h)
    for h in range(KVH):
        pump(1, h)
    before(KVH - 1)
    for h in range(KVH):
        pump(2, h)
    total = middle(0)
    for h in range(1, KVH):
        total += middle(h)
    go1(jnp.sum(total, axis=0, keepdims=True))

    back_step(1, 0)
    back_step(1, 1)
    after(0)
    back_step(1, 2)
    back_step(1, 3)
    go2(end1())
    back_step(0, 0)
    after(1)
    back_step(0, 1)
    after(2)
    back_step(0, 2)
    after(3)
    kv_out = pltpu.make_async_copy(kvg_v, kvg_hbm.at[0], out_sem.at[KVH])
    kv_out.start()
    back_step(0, 3)

    def finish_prompt(h):
        back(0, h).wait_recv()
        both = parts[0, h] + grecv[0, h].astype(F32)
        raw = p_v[:, h * HD : (h + 1) * HD].astype(F32)
        pg_v[:, h * HD : (h + 1) * HD] = norm_backward(raw, unit_factor(raw), ck * both[0]).astype(BF16)
        pg_v[:, KW + h * HD : KW + (h + 1) * HD] = both[1].astype(BF16)

    for h in range(KVH):
        finish_prompt(h)
    p_out = pltpu.make_async_copy(pg_v, pg_hbm.at[0], out_sem.at[KVH + 1])
    p_out.start()
    for k in range(SPAN - 1):
        for h in range(KVH):
            for copy in hop(k, h):
                copy.wait_send()
            back(k, h).wait_send()
    drain1()
    for h in range(KVH):
        q_out(h).wait()
    kv_out.wait()
    summed = end2() * (1.0 / math.sqrt(GS * ZS * YS * CT))
    gains_ref[0:1] = summed / cq
    gains_ref[1:2] = summed / ck
    drain2()
    p_out.wait()


def shards(queries, out_grad, keys_values, prompt_kv, q_gain, k_gain, block_owner, block_start):
    hbm = pl.BlockSpec(memory_space=pltpu.HBM)
    anywhere = pl.BlockSpec(memory_space=pl.ANY)
    vmem = pl.BlockSpec(memory_space=pltpu.VMEM)
    dma = pltpu.SemaphoreType.DMA
    return pl.pallas_call(
        kernel,
        out_shape=(
            jax.ShapeDtypeStruct((1, CT, QW), BF16),
            jax.ShapeDtypeStruct((1, CT, 2 * KW), BF16),
            jax.ShapeDtypeStruct((1, P_SIZE, 2 * KW), BF16),
            jax.ShapeDtypeStruct((2, HD), F32),
        ),
        in_specs=[hbm] * 8,
        out_specs=(anywhere, anywhere, anywhere, vmem),
        scratch_shapes=[
            pltpu.VMEM((CT, QW), BF16),
            pltpu.VMEM((CT, QW), BF16),
            pltpu.VMEM((CT, 2 * KW), BF16),
            pltpu.VMEM((P_SIZE, 2 * KW), BF16),
            pltpu.VMEM((1, HD), F32),
            pltpu.VMEM((1, HD), F32),
            pltpu.SMEM((1, 2), jnp.int32),
            pltpu.SMEM((1, 2), jnp.int32),
            pltpu.VMEM((CT, QW), BF16),
            pltpu.VMEM((CT, 2 * KW), BF16),
            pltpu.VMEM((P_SIZE, 2 * KW), BF16),
            pltpu.VMEM((KVH, 3 * BLK, ROWS), F32),
            pltpu.VMEM((KVH, 3 * BLK, ROWS), F32),
            pltpu.VMEM((KVH, 2, 3 * BLK + 16, ROWS), BF16),
            pltpu.VMEM((SPAN - 1, KVH, 2, P_SIZE, HD), BF16),
            pltpu.VMEM((SPAN - 1, KVH, 2, P_SIZE, HD), F32),
            pltpu.VMEM((SPAN - 1, KVH, 2, P_SIZE, HD), BF16),
            pltpu.VMEM((SPAN - 1, KVH, 2, P_SIZE, HD), BF16),
            pltpu.VMEM((YS * GS, 1, HD), F32),
            pltpu.VMEM((ZS, 1, HD), F32),
            dma((KVH,)),
            dma((KVH,)),
            dma((6,)),
            dma((KVH + 2,)),
            dma((SPAN - 1, KVH, 2)),
            dma((SPAN - 1, KVH, 2)),
            dma((SPAN - 1, KVH)),
            dma((SPAN - 1, KVH)),
            dma((YS * GS,)),
            dma((YS * GS,)),
            dma((ZS,)),
            dma((ZS,)),
        ],
        compiler_params=pltpu.CompilerParams(
            collective_id=0, has_side_effects=True, vmem_limit_bytes=60 * 1024 * 1024
        ),
        name="prefix_attention_grad",
    )(
        queries,
        out_grad,
        keys_values,
        prompt_kv,
        q_gain.reshape(1, HD),
        k_gain.reshape(1, HD),
        block_owner,
        block_start,
    )


def solution(mesh):
    placed = (
        P("group", "dp", None),
        P("group", "dp", None),
        P("group", "dp", None),
        P("group", "dp", None),
        P(),
        P(),
        P("group", "dp"),
        P("group", "dp"),
    )
    return jax.shard_map(
        shards,
        mesh=mesh,
        in_specs=placed,
        out_specs=(P("group", "dp", None), P("group", "dp", None), P("group", "dp", None), P()),
        check_vma=False,
    )
```

time: 64.4 us -> 49 us (0.76)
  Pallas kernels: 55.6 us -> 43.6 us
  local copies, waits for them, and re-layouts: 7.86 us -> 4.56 us
    pallas_call x1, Pallas kernels: 55.6 us -> 43.6 us  [shards(): pl.pallas_call(kernel, out_shape=(jax.ShapeDtypeStruct((1, CT, QW), BF16)...]
    unnamed x20 -> x10, local copies, waits for them, and re-layouts: 7.86 us -> 4.56 us
where the time goes in v2:
time: 49 us; the launch traced here: 48.8 us
  Pallas kernels  43.6 us (89%)
  local copies, waits for them, and re-layouts  4.56 us (9%)
  between operations  0.65 us (1%)
    pallas_call x1, Pallas kernels, shards(): pl.pallas_call(kernel, out_shape=(jax.ShapeDtypeStruct((1, CT, QW), BF16)...  43.6 us
    unnamed x10, local copies, waits for them, and re-layouts  4.56 us

profile of v2, /device:TPU:1, one launch (start us, length us, event | category | flops | bytes accessed | tf_op | source)
XLA Modules:
  0.0 48.8 jit_solution(344063282015861385)
XLA Ops:
  0.6 43.6 %prefix_attention_grad.1 = (bf16[1,128,4096]{2,1,0:T(8,128)(2,1)}, bf16[1,128,1024]{2,1,0:T(8,128)(2,1)}, bf16[1,64,1024]{2,1,0:T(8,128)(2,1)}, f32[2,128]{1,0:T(2,128)}) custom-call(bf16[1,128,4096]{2,1,0:T(8,128)(2,1)} %q_hbm.1, bf16[1,128,4096]{2,1,0:T(8,128)(2,1)} %g_hbm.1, bf16[1,128,1024]{2,1,0:T(8,128)(2,1)} %kv_hbm.1, bf16[1,64,1024]{2,1,0:T(8,128)(2,1)} %p_hbm.1, ...), custom_call_target="tpu_custom_call" | custom-call | tf_op jit(solution)/shard_map/prefix_attention_grad/pallas_call | solution.py:423
  44.2 0.0 copy-start
  44.2 2.3 %copy.16 = bf16[1,128,4096]{2,1,0:T(8,128)(2,1)} copy(bf16[1,128,4096]{2,1,0:T(8,128)(2,1)} %get-tuple-element.8) | data formatting | bytes 2097152
  46.6 0.0 copy-done
  46.6 0.0 copy-start.1
  46.6 0.7 %copy.17 = bf16[1,128,1024]{2,1,0:T(8,128)(2,1)} copy(bf16[1,128,1024]{2,1,0:T(8,128)(2,1)S(1)} %copy-done) | data formatting | bytes 524288
  47.3 0.3 copy-done.1
  47.6 0.0 copy-start.2
  47.6 0.7 %copy.18 = bf16[1,64,1024]{2,1,0:T(8,128)(2,1)} copy(bf16[1,64,1024]{2,1,0:T(8,128)(2,1)S(1)} %copy-done.1) | data formatting | bytes 262144
  48.2 0.0 copy-done.2
  48.2 0.6 %copy.19 = f32[2,128]{1,0:T(2,128)} copy(f32[2,128]{1,0:T(2,128)S(1)} %copy-done.2) | data formatting | bytes 2048
Async XLA Ops:
  44.2 2.3 %copy-start = (bf16[1,128,1024]{2,1,0:T(8,128)(2,1)S(1)}, bf16[1,128,1024]{2,1,0:T(8,128)(2,1)}, u32[]{:S(2)}) copy-start(bf16[1,128,1024]{2,1,0:T(8,128)(2,1)} %get-tuple-element.9) | copy-start | bytes 786436
  46.6 1.0 %copy-start.1 = (bf16[1,64,1024]{2,1,0:T(8,128)(2,1)S(1)}, bf16[1,64,1024]{2,1,0:T(8,128)(2,1)}, u32[]{:S(2)}) copy-start(bf16[1,64,1024]{2,1,0:T(8,128)(2,1)} %get-tuple-element.10) | copy-start | bytes 393220
  47.6 0.7 %copy-start.2 = (f32[2,128]{1,0:T(2,128)S(1)}, f32[2,128]{1,0:T(2,128)}, u32[]{:S(2)}) copy-start(f32[2,128]{1,0:T(2,128)} %get-tuple-element.11) | copy-start | bytes 3076

commit v3 on v2

--- a/solution.py
+++ b/solution.py
@@ -58,11 +58,11 @@
 
 def kernel(
     q_hbm, g_hbm, kv_hbm, p_hbm, qgain_hbm, kgain_hbm, owner_hbm, start_hbm,
-    qg_hbm, kvg_hbm, pg_hbm, gains_ref,
-    q_v, g_v, kv_v, p_v, qgain, kgain, owner, start, qg_v, kvg_v, pg_v,
+    qg_v, kvg_v, pg_v, gains_ref,
+    q_v, g_v, kv_v, own, qgain, kgain, owner, start,
     e_v, d_v, lhs_v, cand, parts, gsend, grecv, ar1, ar2,
-    q_sem, g_sem, small_sem, out_sem, f_send, f_recv, b_send, b_recv,
-    a1_send, a1_recv, a2_send, a2_recv,
+    q_sem, g_sem, small_sem, own_sem, f_send, f_recv, b_send, b_recv,
+    a1_send, a1_recv, a2_send, a2_recv, known,
 ):
     me = lax.axis_index("dp")
     grp = lax.axis_index("group")
@@ -95,10 +95,29 @@
     )
     z_order = sorted(range(1, ZS), key=lambda j: -ring_steps(j, ZS))
 
+    def x_peer(j):
+        return (me, lax.rem(grp + 2 * j, GS))
+
+    def y_peer(j):
+        return (lax.rem(my_y + j, YS) * ZS + my_z, grp)
+
+    other_core = (me, grp + 1 - 2 * lax.rem(grp, 2))
+    beside = [y_peer(1), y_peer(YS - 1), x_peer(1), x_peer(GS // 2 - 1), other_core]
+    rounds = [
+        beside + [z_peer(1), z_peer(ZS - 1)],
+        beside + [y_peer(2), x_peer(2), z_peer(2), z_peer(ZS - 2)],
+        [other_core, z_peer(4), z_peer(ZS - 4)],
+    ]
+
+    def tell(i):
+        for peer in rounds[i]:
+            pl.semaphore_signal(known.at[i], inc=1, device_id=peer, device_id_type=MESH)
+
+    def hear(i):
+        pl.semaphore_wait(known.at[i], len(rounds[i]))
+
     barrier = pltpu.get_barrier_semaphore()
-    partners = [(right, grp), (left, grp)]
-    partners += [z_peer(j) for j in z_order]
-    partners += [plane_peer(j) for j in plane_order]
+    partners = [(right, grp), (left, grp)] + rounds[0]
     for peer in partners:
         pl.semaphore_signal(barrier, inc=1, device_id=peer, device_id_type=MESH)
 
@@ -111,48 +130,37 @@
                 (kgain_hbm, kgain),
                 (owner_hbm, owner),
                 (start_hbm, start),
-                (p_hbm.at[0], p_v),
             ]
         )
+    ]
+    own_loads = [
+        pltpu.make_async_copy(
+            p_hbm.at[0, :, pl.ds(part * KW + h * HD, HD)], own.at[h, part], own_sem.at[h, part]
+        )
+        for h in range(KVH)
+        for part in range(2)
     ]
     q_loads, g_loads = [], []
     for h in range(KVH):
         cols = pl.ds(h * MEMBERS * HD, MEMBERS * HD)
         q_loads.append(pltpu.make_async_copy(q_hbm.at[0, :, cols], q_v.at[:, cols], q_sem.at[h]))
         g_loads.append(pltpu.make_async_copy(g_hbm.at[0, :, cols], g_v.at[:, cols], g_sem.at[h]))
-    for load in small[:3] + [q_loads[0], g_loads[0]] + small[3:] + q_loads[1:] + g_loads[1:]:
+    for load in own_loads + small + [q_loads[0], g_loads[0]] + q_loads[1:] + g_loads[1:]:
         load.start()
 
     def hop(k, h):
-        copies = []
-        for part in range(2):
-            if k == 0:
-                src = p_hbm.at[0, :, pl.ds(part * KW + h * HD, HD)]
-            else:
-                src = cand.at[k - 1, h, part]
-            copies.append(
-                pltpu.make_async_remote_copy(
-                    src_ref=src,
-                    dst_ref=cand.at[k, h, part],
-                    send_sem=f_send.at[k, h, part],
-                    recv_sem=f_recv.at[k, h, part],
-                    device_id=(right, grp),
-                    device_id_type=MESH,
-                )
-            )
-        return copies
-
-    def send(k, h):
-        for copy in hop(k, h):
-            copy.start()
-
-    def arrive(k, h):
-        for copy in hop(k, h):
-            copy.wait_recv()
+        return pltpu.make_async_remote_copy(
+            src_ref=own.at[h] if k == 0 else cand.at[k - 1, h],
+            dst_ref=cand.at[k, h],
+            send_sem=f_send.at[k, h],
+            recv_sem=f_recv.at[k, h],
+            device_id=(right, grp),
+            device_id_type=MESH,
+        )
 
     def pump(k, h):
-        arrive(k - 1, h)
-        send(k, h)
+        hop(k - 1, h).wait_recv()
+        hop(k, h).start()
 
     def back(k, h):
         return pltpu.make_async_remote_copy(
@@ -201,9 +209,12 @@
     )
     go2, end2, drain2 = exchange(ar2, my_z, z_order, z_peer, z_slot, a2_send, a2_recv)
 
+    for load in own_loads:
+        load.wait()
     pl.semaphore_wait(barrier, len(partners))
     for h in range(KVH):
-        send(0, h)
+        hop(0, h).start()
+    tell(0)
 
     key_at = lax.broadcasted_iota(jnp.int32, (BLK, ROWS), 0)
     row_at = lax.rem(lax.broadcasted_iota(jnp.int32, (BLK, ROWS), 1), BLK)
@@ -268,17 +279,16 @@
             stats[h, n] = (s, over_keys(e), over_keys(e * d), over_keys(er), over_keys(er * d))
 
     def pick(slot, h, part):
-        c = part * KW + h * HD
-        own = p_v[:, c : c + HD].astype(F32)
+        mine = own[h, part].astype(F32)
         got = [cand[k, h, part].astype(F32) for k in range(SPAN - 1)]
         return jnp.where(
-            slot == 0, own, jnp.where(slot == 1, got[0], jnp.where(slot == 2, got[1], got[2]))
+            slot == 0, mine, jnp.where(slot == 1, got[0], jnp.where(slot == 2, got[1], got[2]))
         )
 
     kept = {}
 
     def middle(h):
-        arrive(SPAN - 2, h)
+        hop(SPAN - 2, h).wait_recv()
         full_l = local_keys(h)[2]
         k_b = full_l.astype(BF16)
         d_p, dks, dvs = [], [], []
@@ -336,17 +346,13 @@
         back(SPAN - 2, h).start()
         dk = jnp.concatenate([dks[0] + dks[1][:BLK], dks[1][BLK:]], axis=0)
         dv = jnp.concatenate([dvs[0] + dvs[1][:BLK], dvs[1][BLK:]], axis=0)
-        kvg_v[:, KW + h * HD : KW + (h + 1) * HD] = dv.astype(BF16)
+        kvg_v[0, :, KW + h * HD : KW + (h + 1) * HD] = dv.astype(BF16)
         kept[h] = dk
         return total + fold8(full_l * dk)
 
-    def q_out(h):
-        cols = pl.ds(h * MEMBERS * HD, MEMBERS * HD)
-        return pltpu.make_async_copy(qg_v.at[:, cols], qg_hbm.at[0, :, cols], out_sem.at[h])
-
     def after(h):
         raw_l, inverse, _ = local_keys(h)
-        kvg_v[:, h * HD : (h + 1) * HD] = norm_backward(raw_l, inverse, cqk * kept[h]).astype(BF16)
+        kvg_v[0, :, h * HD : (h + 1) * HD] = norm_backward(raw_l, inverse, cqk * kept[h]).astype(BF16)
         for n in range(2):
             count = (n + 2) * BLK
             rhs = jnp.concatenate(
@@ -357,19 +363,24 @@
             dx = (z[:, :HD] - x * z[:, HD:]).astype(BF16)
             for m in range(MEMBERS):
                 c = (h * MEMBERS + m) * HD
-                qg_v[n * BLK : (n + 1) * BLK, c : c + HD] = dx[m * BLK : (m + 1) * BLK]
-        q_out(h).start()
-
-    for h in range(KVH - 1):
-        before(h)
+                qg_v[0, n * BLK : (n + 1) * BLK, c : c + HD] = dx[m * BLK : (m + 1) * BLK]
+
+    before(0)
+    hear(0)
+    tell(1)
+    before(1)
+    before(2)
     for h in range(KVH):
         pump(1, h)
-    before(KVH - 1)
+    hear(1)
+    tell(2)
+    before(3)
     for h in range(KVH):
         pump(2, h)
     total = middle(0)
     for h in range(1, KVH):
         total += middle(h)
+    hear(2)
     go1(jnp.sum(total, axis=0, keepdims=True))
 
     back_step(1, 0)
@@ -384,35 +395,26 @@
     after(2)
     back_step(0, 2)
     after(3)
-    kv_out = pltpu.make_async_copy(kvg_v, kvg_hbm.at[0], out_sem.at[KVH])
-    kv_out.start()
     back_step(0, 3)
 
     def finish_prompt(h):
         back(0, h).wait_recv()
         both = parts[0, h] + grecv[0, h].astype(F32)
-        raw = p_v[:, h * HD : (h + 1) * HD].astype(F32)
-        pg_v[:, h * HD : (h + 1) * HD] = norm_backward(raw, unit_factor(raw), ck * both[0]).astype(BF16)
-        pg_v[:, KW + h * HD : KW + (h + 1) * HD] = both[1].astype(BF16)
+        raw = own[h, 0].astype(F32)
+        pg_v[0, :, h * HD : (h + 1) * HD] = norm_backward(raw, unit_factor(raw), ck * both[0]).astype(BF16)
+        pg_v[0, :, KW + h * HD : KW + (h + 1) * HD] = both[1].astype(BF16)
 
     for h in range(KVH):
         finish_prompt(h)
-    p_out = pltpu.make_async_copy(pg_v, pg_hbm.at[0], out_sem.at[KVH + 1])
-    p_out.start()
     for k in range(SPAN - 1):
         for h in range(KVH):
-            for copy in hop(k, h):
-                copy.wait_send()
+            hop(k, h).wait_send()
             back(k, h).wait_send()
     drain1()
-    for h in range(KVH):
-        q_out(h).wait()
-    kv_out.wait()
     summed = end2() * (1.0 / math.sqrt(GS * ZS * YS * CT))
     gains_ref[0:1] = summed / cq
     gains_ref[1:2] = summed / ck
     drain2()
-    p_out.wait()
 
 
 def shards(queries, out_grad, keys_values, prompt_kv, q_gain, k_gain, block_owner, block_start):
@@ -420,28 +422,25 @@
     anywhere = pl.BlockSpec(memory_space=pl.ANY)
     vmem = pl.BlockSpec(memory_space=pltpu.VMEM)
     dma = pltpu.SemaphoreType.DMA
-    return pl.pallas_call(
+    held = pl.pallas_call(
         kernel,
         out_shape=(
-            jax.ShapeDtypeStruct((1, CT, QW), BF16),
-            jax.ShapeDtypeStruct((1, CT, 2 * KW), BF16),
-            jax.ShapeDtypeStruct((1, P_SIZE, 2 * KW), BF16),
-            jax.ShapeDtypeStruct((2, HD), F32),
+            pltpu.VMEM((1, CT, QW), BF16),
+            pltpu.VMEM((1, CT, 2 * KW), BF16),
+            pltpu.VMEM((1, P_SIZE, 2 * KW), BF16),
+            pltpu.VMEM((2, HD), F32),
         ),
         in_specs=[hbm] * 8,
-        out_specs=(anywhere, anywhere, anywhere, vmem),
+        out_specs=(vmem, vmem, vmem, vmem),
         scratch_shapes=[
             pltpu.VMEM((CT, QW), BF16),
             pltpu.VMEM((CT, QW), BF16),
             pltpu.VMEM((CT, 2 * KW), BF16),
-            pltpu.VMEM((P_SIZE, 2 * KW), BF16),
+            pltpu.VMEM((KVH, 2, P_SIZE, HD), BF16),
             pltpu.VMEM((1, HD), F32),
             pltpu.VMEM((1, HD), F32),
             pltpu.SMEM((1, 2), jnp.int32),
             pltpu.SMEM((1, 2), jnp.int32),
-            pltpu.VMEM((CT, QW), BF16),
-            pltpu.VMEM((CT, 2 * KW), BF16),
-            pltpu.VMEM((P_SIZE, 2 * KW), BF16),
             pltpu.VMEM((KVH, 3 * BLK, ROWS), F32),
             pltpu.VMEM((KVH, 3 * BLK, ROWS), F32),
             pltpu.VMEM((KVH, 2, 3 * BLK + 16, ROWS), BF16),
@@ -453,16 +452,17 @@
             pltpu.VMEM((ZS, 1, HD), F32),
             dma((KVH,)),
             dma((KVH,)),
-            dma((6,)),
-            dma((KVH + 2,)),
-            dma((SPAN - 1, KVH, 2)),
-            dma((SPAN - 1, KVH, 2)),
+            dma((5,)),
+            dma((KVH, 2)),
+            dma((SPAN - 1, KVH)),
+            dma((SPAN - 1, KVH)),
             dma((SPAN - 1, KVH)),
             dma((SPAN - 1, KVH)),
             dma((YS * GS,)),
             dma((YS * GS,)),
             dma((ZS,)),
             dma((ZS,)),
+            pltpu.SemaphoreType.REGULAR((3,)),
         ],
         compiler_params=pltpu.CompilerParams(
             collective_id=0, has_side_effects=True, vmem_limit_bytes=60 * 1024 * 1024
@@ -478,6 +478,29 @@
         block_owner,
         block_start,
     )
+    return pl.pallas_call(
+        hand_over,
+        out_shape=tuple(jax.ShapeDtypeStruct(a.shape, a.dtype) for a in held),
+        in_specs=[vmem] * 4,
+        out_specs=(anywhere,) * 4,
+        scratch_shapes=[dma((KVH * 2 + 3,))],
+        compiler_params=pltpu.CompilerParams(vmem_limit_bytes=8 * 1024 * 1024),
+        name="hand_over",
+    )(*held)
+
+
+def hand_over(qg, kvg, pg, gains, qg_out, kvg_out, pg_out, gains_out, sem):
+    copies = []
+    for i in range(2 * KVH):
+        rows = pl.ds(i * 16, 16)
+        copies.append(pltpu.make_async_copy(qg.at[0, rows], qg_out.at[0, rows], sem.at[i]))
+    copies.append(pltpu.make_async_copy(kvg, kvg_out, sem.at[2 * KVH]))
+    copies.append(pltpu.make_async_copy(pg, pg_out, sem.at[2 * KVH + 1]))
+    copies.append(pltpu.make_async_copy(gains, gains_out, sem.at[2 * KVH + 2]))
+    for copy in copies:
+        copy.start()
+    for copy in copies:
+        copy.wait()
 
 
 def solution(mesh):

time: 49 us -> 40.9 us (0.83)
  local copies, waits for them, and re-layouts: 4.56 us -> 0 us
  Pallas kernels: 43.6 us -> 40.1 us
    unnamed x10 -> x0, local copies, waits for them, and re-layouts: 4.56 us -> none
    pallas_call x1 -> x2, Pallas kernels: 43.6 us -> 40.1 us  [the longest x1 38.9 us: shards(): pl.pallas_call(kernel, out_shape=(pltpu.VMEM((1, CT, QW), BF16), pltpu.VM...]
where the time goes in v3:
time: 40.9 us; the launch traced here: 40.7 us
  Pallas kernels  40.1 us (98%)
  between operations  0.64 us (2%)
    pallas_call x1, Pallas kernels, shards(): pl.pallas_call(kernel, out_shape=(pltpu.VMEM((1, CT, QW), BF16), pltpu.VM...  38.9 us
    pallas_call x1, Pallas kernels, shards(): pl.pallas_call(hand_over, out_shape=tuple((jax.ShapeDtypeStruct(a.shape,...  1.19 us

profile of v3, /device:TPU:1, one launch (start us, length us, event | category | flops | bytes accessed | tf_op | source)
XLA Modules:
  0.0 40.7 jit_solution(17307578031496514279)
XLA Ops:
  0.6 38.9 %prefix_attention_grad.1 = (bf16[1,128,4096]{2,1,0:T(8,128)(2,1)S(1)}, bf16[1,128,1024]{2,1,0:T(8,128)(2,1)S(1)}, bf16[1,64,1024]{2,1,0:T(8,128)(2,1)S(1)}, f32[2,128]{1,0:T(2,128)S(1)}) custom-call(bf16[1,128,4096]{2,1,0:T(8,128)(2,1)} %q_hbm.1, bf16[1,128,4096]{2,1,0:T(8,128)(2,1)} %g_hbm.1, bf16[1,128,1024]{2,1,0:T(8,128)(2,1)} %kv_hbm.1, ...), custom_call_target="tpu_custom_call" | custom-call | tf_op jit(solution)/shard_map/prefix_attention_grad/pallas_call | solution.py:425
  39.5 1.2 %hand_over.1 = (bf16[1,128,4096]{2,1,0:T(8,128)(2,1)}, bf16[1,128,1024]{2,1,0:T(8,128)(2,1)}, bf16[1,64,1024]{2,1,0:T(8,128)(2,1)}, f32[2,128]{1,0:T(2,128)}) custom-call(bf16[1,128,4096]{2,1,0:T(8,128)(2,1)S(1)} %get-tuple-element.8.qg, bf16[1,128,1024]{2,1,0:T(8,128)(2,1)S(1)} %get-tuple-element.9.kvg, bf16[1,64,1024]{2,1,0:T(8,128)(2,1)S(1)} %get-tuple-element.10.pg, ...), custom_call_target="tpu_custom_call" | custom-call | tf_op jit(solution)/shard_map/hand_over/pallas_call | solution.py:481

commit v4 on v3

--- a/solution.py
+++ b/solution.py
@@ -22,6 +22,7 @@
 NORM_EPS = 1e-06
 SCALE = HD**-0.5
 LOG2E = math.log2(math.e)
+LATE = 2
 ZS = 16
 YS = 4
 GS = 8
@@ -60,7 +61,7 @@
     q_hbm, g_hbm, kv_hbm, p_hbm, qgain_hbm, kgain_hbm, owner_hbm, start_hbm,
     qg_v, kvg_v, pg_v, gains_ref,
     q_v, g_v, kv_v, own, qgain, kgain, owner, start,
-    e_v, d_v, lhs_v, cand, parts, gsend, grecv, ar1, ar2,
+    e_v, d_v, lhs_v, cand, parts, gsend, grecv, prob_v, ar1, ar2,
     q_sem, g_sem, small_sem, own_sem, f_send, f_recv, b_send, b_recv,
     a1_send, a1_recv, a2_send, a2_recv, known,
 ):
@@ -76,15 +77,8 @@
         y, g = plane_at(j)
         return (y * ZS + my_z, g)
 
-    def plane_slot(j):
-        y, g = plane_at(j)
-        return y * GS + g
-
     def z_peer(j):
         return (my_y * ZS + lax.rem(my_z + j, ZS), grp)
-
-    def z_slot(j):
-        return lax.rem(my_z + j, ZS)
 
     def ring_steps(j, size):
         return min(j, size - j)
@@ -162,13 +156,16 @@
         hop(k - 1, h).wait_recv()
         hop(k, h).start()
 
+    left2 = lax.rem(me + ZS * YS - 2, ZS * YS)
+
     def back(k, h):
+        target = left2 if k == 1 and h >= LATE else left
         return pltpu.make_async_remote_copy(
             src_ref=gsend.at[k, h],
             dst_ref=grecv.at[k, h],
             send_sem=b_send.at[k, h],
             recv_sem=b_recv.at[k, h],
-            device_id=(left, grp),
+            device_id=(target, grp),
             device_id_type=MESH,
         )
 
@@ -177,13 +174,13 @@
         gsend[k, h] = (parts[k + 1, h] + grecv[k + 1, h].astype(F32)).astype(BF16)
         back(k, h).start()
 
-    def exchange(buf, mine, order, peer_of, slot_of, send_sem, recv_sem):
+    def exchange(buf, mine, order, peer_of, send_sem, recv_sem):
         def copy(j, slot):
             return pltpu.make_async_remote_copy(
                 src_ref=buf.at[slot],
                 dst_ref=buf.at[slot],
                 send_sem=send_sem.at[j],
-                recv_sem=recv_sem.at[slot],
+                recv_sem=recv_sem,
                 device_id=peer_of(j),
                 device_id_type=MESH,
             )
@@ -194,8 +191,8 @@
                 copy(j, mine).start()
 
         def finish():
-            for j in reversed(order):
-                copy(j, slot_of(j)).wait_recv()
+            others = buf.at[pl.ds(0, len(order))]
+            pltpu.make_async_copy(others, others, recv_sem).wait()
             return jnp.sum(buf[...], axis=0)
 
         def drain():
@@ -205,9 +202,9 @@
         return go, finish, drain
 
     go1, end1, drain1 = exchange(
-        ar1, my_y * GS + grp, plane_order, plane_peer, plane_slot, a1_send, a1_recv
-    )
-    go2, end2, drain2 = exchange(ar2, my_z, z_order, z_peer, z_slot, a2_send, a2_recv)
+        ar1, my_y * GS + grp, plane_order, plane_peer, a1_send, a1_recv
+    )
+    go2, end2, drain2 = exchange(ar2, my_z, z_order, z_peer, a2_send, a2_recv)
 
     for load in own_loads:
         load.wait()
@@ -291,7 +288,7 @@
         hop(SPAN - 2, h).wait_recv()
         full_l = local_keys(h)[2]
         k_b = full_l.astype(BF16)
-        d_p, dks, dvs = [], [], []
+        dks, d_p = [], []
         total = jnp.zeros((8, HD), F32)
         for n in range(2):
             count = (n + 1) * BLK
@@ -323,32 +320,48 @@
             )
             prob = jnp.concatenate([prob_l.astype(BF16), prob_p.astype(BF16)], axis=0)
             dk = nn(d2, x)
-            dv = nn(prob, g)
+            if h >= LATE:
+                prob_v[h - LATE, n, : count + BLK] = prob
+            else:
+                kept["prob", n] = prob
             fac = s * s * s * m * (SCALE / HD)
             hi = fac.astype(BF16).astype(F32)
             extra = jnp.where(sub16 == 0, hi, jnp.where(sub16 == 1, fac - hi, 0.0)).astype(BF16)
             lhs_v[h, n, : count + BLK] = d2
             lhs_v[h, n, count + BLK : count + BLK + 16] = extra
             kept[h, n] = jnp.concatenate([k_b[:count], p_b], axis=0)
-            d_p.append((cq * dk[count:], dv[count:]))
+            d_p.append(cq * dk[count:])
             dks.append(dk[:count])
+            total += fold8(full * dk[count:])
+        for k in range(SPAN):
+            term = jnp.where(slots[0] == k, d_p[0], 0.0) + jnp.where(slots[1] == k, d_p[1], 0.0)
+            put_part(k, h, 0, term)
+        dk = jnp.concatenate([dks[0] + dks[1][:BLK], dks[1][BLK:]], axis=0)
+        kept[h] = dk
+        return total + fold8(full_l * dk)
+
+    def put_part(k, h, part, term):
+        if k == SPAN - 1 or (k == 1 and h >= LATE):
+            gsend[k - 1, h, part] = term.astype(BF16)
+        else:
+            parts[k, h, part] = term
+
+    def values(h):
+        dvs, d_p = [], []
+        for n in range(2):
+            count = (n + 1) * BLK
+            prob = prob_v[h - LATE, n, : count + BLK] if h >= LATE else kept["prob", n]
+            dv = nn(prob, rows_of(g_v, n, h))
             dvs.append(dv[:count])
-            total += fold8(full * dk[count:])
-        for part in range(2):
-            for k in range(SPAN):
-                term = jnp.where(slots[0] == k, d_p[0][part], 0.0) + jnp.where(
-                    slots[1] == k, d_p[1][part], 0.0
-                )
-                if k == SPAN - 1:
-                    gsend[k - 1, h, part] = term.astype(BF16)
-                else:
-                    parts[k, h, part] = term
+            d_p.append(dv[count:])
+        for k in range(SPAN):
+            term = jnp.where(slots[0] == k, d_p[0], 0.0) + jnp.where(slots[1] == k, d_p[1], 0.0)
+            put_part(k, h, 1, term)
         back(SPAN - 2, h).start()
-        dk = jnp.concatenate([dks[0] + dks[1][:BLK], dks[1][BLK:]], axis=0)
+        if h >= LATE:
+            back(0, h).start()
         dv = jnp.concatenate([dvs[0] + dvs[1][:BLK], dvs[1][BLK:]], axis=0)
         kvg_v[0, :, KW + h * HD : KW + (h + 1) * HD] = dv.astype(BF16)
-        kept[h] = dk
-        return total + fold8(full_l * dk)
 
     def after(h):
         raw_l, inverse, _ = local_keys(h)
@@ -370,36 +383,43 @@
     tell(1)
     before(1)
     before(2)
-    for h in range(KVH):
-        pump(1, h)
+    pump(1, 0)
+    pump(1, 1)
     hear(1)
     tell(2)
+    pump(1, 2)
+    pump(1, 3)
     before(3)
     for h in range(KVH):
         pump(2, h)
     total = middle(0)
-    for h in range(1, KVH):
-        total += middle(h)
+    values(0)
+    total += middle(1)
+    values(1)
+    total += middle(2)
+    values(2)
+    total += middle(3)
     hear(2)
     go1(jnp.sum(total, axis=0, keepdims=True))
-
+    values(3)
     back_step(1, 0)
     back_step(1, 1)
     after(0)
     back_step(1, 2)
+    after(1)
+    go2(end1())
     back_step(1, 3)
-    go2(end1())
     back_step(0, 0)
-    after(1)
     back_step(0, 1)
     after(2)
-    back_step(0, 2)
     after(3)
-    back_step(0, 3)
 
     def finish_prompt(h):
         back(0, h).wait_recv()
         both = parts[0, h] + grecv[0, h].astype(F32)
+        if h >= LATE:
+            back(1, h).wait_recv()
+            both = both + grecv[1, h].astype(F32)
         raw = own[h, 0].astype(F32)
         pg_v[0, :, h * HD : (h + 1) * HD] = norm_backward(raw, unit_factor(raw), ck * both[0]).astype(BF16)
         pg_v[0, :, KW + h * HD : KW + (h + 1) * HD] = both[1].astype(BF16)
@@ -448,6 +468,7 @@
             pltpu.VMEM((SPAN - 1, KVH, 2, P_SIZE, HD), F32),
             pltpu.VMEM((SPAN - 1, KVH, 2, P_SIZE, HD), BF16),
             pltpu.VMEM((SPAN - 1, KVH, 2, P_SIZE, HD), BF16),
+            pltpu.VMEM((KVH - LATE, 2, 3 * BLK, ROWS), BF16),
             pltpu.VMEM((YS * GS, 1, HD), F32),
             pltpu.VMEM((ZS, 1, HD), F32),
             dma((KVH,)),
@@ -459,9 +480,9 @@
             dma((SPAN - 1, KVH)),
             dma((SPAN - 1, KVH)),
             dma((YS * GS,)),
-            dma((YS * GS,)),
+            dma,
             dma((ZS,)),
-            dma((ZS,)),
+            dma,
             pltpu.SemaphoreType.REGULAR((3,)),
         ],
         compiler_params=pltpu.CompilerParams(

time: 40.9 us -> 40.3 us (0.985)
  Pallas kernels: 40.1 us -> 39.6 us
    pallas_call x1, Pallas kernels: 38.9 us -> 38.4 us  [shards(): pl.pallas_call(kernel, out_shape=(pltpu.VMEM((1, CT, QW), BF16), pltpu.VM...]
where the time goes in v4:
time: 40.3 us; the launch traced here: 40.2 us
  Pallas kernels  39.6 us (98%)
  between operations  0.64 us (2%)
    pallas_call x1, Pallas kernels, shards(): pl.pallas_call(kernel, out_shape=(pltpu.VMEM((1, CT, QW), BF16), pltpu.VM...  38.4 us
    pallas_call x1, Pallas kernels, shards(): pl.pallas_call(hand_over, out_shape=tuple((jax.ShapeDtypeStruct(a.shape,...  1.19 us

profile of v4, /device:TPU:1, one launch (start us, length us, event | category | flops | bytes accessed | tf_op | source)
XLA Modules:
  0.0 40.2 jit_solution(10478907969479007308)
XLA Ops:
  0.6 38.4 %prefix_attention_grad.1 = (bf16[1,128,4096]{2,1,0:T(8,128)(2,1)S(1)}, bf16[1,128,1024]{2,1,0:T(8,128)(2,1)S(1)}, bf16[1,64,1024]{2,1,0:T(8,128)(2,1)S(1)}, f32[2,128]{1,0:T(2,128)S(1)}) custom-call(bf16[1,128,4096]{2,1,0:T(8,128)(2,1)} %q_hbm.1, bf16[1,128,4096]{2,1,0:T(8,128)(2,1)} %g_hbm.1, bf16[1,128,1024]{2,1,0:T(8,128)(2,1)} %kv_hbm.1, ...), custom_call_target="tpu_custom_call" | custom-call | tf_op jit(solution)/shard_map/prefix_attention_grad/pallas_call | solution.py:445
  39.0 1.2 %hand_over.1 = (bf16[1,128,4096]{2,1,0:T(8,128)(2,1)}, bf16[1,128,1024]{2,1,0:T(8,128)(2,1)}, bf16[1,64,1024]{2,1,0:T(8,128)(2,1)}, f32[2,128]{1,0:T(2,128)}) custom-call(bf16[1,128,4096]{2,1,0:T(8,128)(2,1)S(1)} %get-tuple-element.8.qg, bf16[1,128,1024]{2,1,0:T(8,128)(2,1)S(1)} %get-tuple-element.9.kvg, bf16[1,64,1024]{2,1,0:T(8,128)(2,1)S(1)} %get-tuple-element.10.pg, ...), custom_call_target="tpu_custom_call" | custom-call | tf_op jit(solution)/shard_map/hand_over/pallas_call | solution.py:502

commit v5 on v4

--- a/solution.py
+++ b/solution.py
@@ -60,7 +60,7 @@
 def kernel(
     q_hbm, g_hbm, kv_hbm, p_hbm, qgain_hbm, kgain_hbm, owner_hbm, start_hbm,
     qg_v, kvg_v, pg_v, gains_ref,
-    q_v, g_v, kv_v, own, qgain, kgain, owner, start,
+    q_v, g_v, kv_v, own, own_raw, qgain, kgain, owner, start,
     e_v, d_v, lhs_v, cand, parts, gsend, grecv, prob_v, ar1, ar2,
     q_sem, g_sem, small_sem, own_sem, f_send, f_recv, b_send, b_recv,
     a1_send, a1_recv, a2_send, a2_recv, known,
@@ -208,8 +208,17 @@
 
     for load in own_loads:
         load.wait()
-    pl.semaphore_wait(barrier, len(partners))
+    small[1].wait()
+    small[2].wait()
+    cq = qgain[...]
+    ck = kgain[...]
+    cqk = cq * ck
     for h in range(KVH):
+        raw = own[h, 0].astype(F32)
+        own_raw[h] = own[h, 0]
+        own[h, 0] = (raw * unit_factor(raw) * cqk).astype(BF16)
+        if h == 0:
+            pl.semaphore_wait(barrier, len(partners))
         hop(0, h).start()
     tell(0)
 
@@ -225,11 +234,8 @@
         ],
         axis=1,
     )
-    for load in small:
+    for load in small[:1] + small[3:]:
         load.wait()
-    cq = qgain[...]
-    ck = kgain[...]
-    cqk = cq * ck
     slots = (me - owner[0, 0], me - owner[0, 1])
     same = jnp.where((start[0, 1] == 1) | (owner[0, 0] != owner[0, 1]), 0.0, 1.0).astype(F32)
 
@@ -293,9 +299,7 @@
         for n in range(2):
             count = (n + 1) * BLK
             at = n * BLK
-            praw = pick(slots[n], h, 0)
-            full = praw * unit_factor(praw) * cqk
-            p_b = full.astype(BF16)
+            p_b = pick(slots[n], h, 0).astype(BF16)
             w_b = pick(slots[n], h, 1).astype(BF16)
             x = rows_of(q_v, n, h)
             g = rows_of(g_v, n, h)
@@ -332,7 +336,7 @@
             kept[h, n] = jnp.concatenate([k_b[:count], p_b], axis=0)
             d_p.append(cq * dk[count:])
             dks.append(dk[:count])
-            total += fold8(full * dk[count:])
+            total += fold8(p_b.astype(F32) * dk[count:])
         for k in range(SPAN):
             term = jnp.where(slots[0] == k, d_p[0], 0.0) + jnp.where(slots[1] == k, d_p[1], 0.0)
             put_part(k, h, 0, term)
@@ -420,7 +424,7 @@
         if h >= LATE:
             back(1, h).wait_recv()
             both = both + grecv[1, h].astype(F32)
-        raw = own[h, 0].astype(F32)
+        raw = own_raw[h].astype(F32)
         pg_v[0, :, h * HD : (h + 1) * HD] = norm_backward(raw, unit_factor(raw), ck * both[0]).astype(BF16)
         pg_v[0, :, KW + h * HD : KW + (h + 1) * HD] = both[1].astype(BF16)
 
@@ -457,6 +461,7 @@
             pltpu.VMEM((CT, QW), BF16),
             pltpu.VMEM((CT, 2 * KW), BF16),
             pltpu.VMEM((KVH, 2, P_SIZE, HD), BF16),
+            pltpu.VMEM((KVH, P_SIZE, HD), BF16),
             pltpu.VMEM((1, HD), F32),
             pltpu.VMEM((1, HD), F32),
             pltpu.SMEM((1, 2), jnp.int32),
@@ -504,20 +509,15 @@
         out_shape=tuple(jax.ShapeDtypeStruct(a.shape, a.dtype) for a in held),
         in_specs=[vmem] * 4,
         out_specs=(anywhere,) * 4,
-        scratch_shapes=[dma((KVH * 2 + 3,))],
+        scratch_shapes=[dma((4,))],
         compiler_params=pltpu.CompilerParams(vmem_limit_bytes=8 * 1024 * 1024),
         name="hand_over",
     )(*held)
 
 
 def hand_over(qg, kvg, pg, gains, qg_out, kvg_out, pg_out, gains_out, sem):
-    copies = []
-    for i in range(2 * KVH):
-        rows = pl.ds(i * 16, 16)
-        copies.append(pltpu.make_async_copy(qg.at[0, rows], qg_out.at[0, rows], sem.at[i]))
-    copies.append(pltpu.make_async_copy(kvg, kvg_out, sem.at[2 * KVH]))
-    copies.append(pltpu.make_async_copy(pg, pg_out, sem.at[2 * KVH + 1]))
-    copies.append(pltpu.make_async_copy(gains, gains_out, sem.at[2 * KVH + 2]))
+    pairs = [(qg, qg_out), (kvg, kvg_out), (pg, pg_out), (gains, gains_out)]
+    copies = [pltpu.make_async_copy(src, dst, sem.at[i]) for i, (src, dst) in enumerate(pairs)]
     for copy in copies:
         copy.start()
     for copy in copies:

time: 40.3 us -> 40.3 us (level)
  no operation moved by 1% of the time
where the time goes in v5:
time: 40.3 us; the launch traced here: 40.2 us
  Pallas kernels  39.6 us (98%)
  between operations  0.64 us (2%)
    pallas_call x1, Pallas kernels, shards(): pl.pallas_call(kernel, out_shape=(pltpu.VMEM((1, CT, QW), BF16), pltpu.VM...  38.4 us
    pallas_call x1, Pallas kernels, shards(): pl.pallas_call(hand_over, out_shape=tuple((jax.ShapeDtypeStruct(a.shape,...  1.13 us

profile of v5, /device:TPU:1, one launch (start us, length us, event | category | flops | bytes accessed | tf_op | source)
XLA Modules:
  0.0 40.2 jit_solution(18343277871197097010)
XLA Ops:
  0.6 38.4 %prefix_attention_grad.1 = (bf16[1,128,4096]{2,1,0:T(8,128)(2,1)S(1)}, bf16[1,128,1024]{2,1,0:T(8,128)(2,1)S(1)}, bf16[1,64,1024]{2,1,0:T(8,128)(2,1)S(1)}, f32[2,128]{1,0:T(2,128)S(1)}) custom-call(bf16[1,128,4096]{2,1,0:T(8,128)(2,1)} %q_hbm.1, bf16[1,128,4096]{2,1,0:T(8,128)(2,1)} %g_hbm.1, bf16[1,128,1024]{2,1,0:T(8,128)(2,1)} %kv_hbm.1, ...), custom_call_target="tpu_custom_call" | custom-call | tf_op jit(solution)/shard_map/prefix_attention_grad/pallas_call | solution.py:449
  39.1 1.1 %hand_over.1 = (bf16[1,128,4096]{2,1,0:T(8,128)(2,1)}, bf16[1,128,1024]{2,1,0:T(8,128)(2,1)}, bf16[1,64,1024]{2,1,0:T(8,128)(2,1)}, f32[2,128]{1,0:T(2,128)}) custom-call(bf16[1,128,4096]{2,1,0:T(8,128)(2,1)S(1)} %get-tuple-element.8.qg, bf16[1,128,1024]{2,1,0:T(8,128)(2,1)S(1)} %get-tuple-element.9.kvg, bf16[1,64,1024]{2,1,0:T(8,128)(2,1)S(1)} %get-tuple-element.10.pg, ...), custom_call_target="tpu_custom_call" | custom-call | tf_op jit(solution)/shard_map/hand_over/pallas_call | solution.py:507
